TPU v7x, 32 devices: a whole 2x2x4 slice. The times are simulated.
32 devices in a mesh: seq: 4 (over x, core), band: 8 (over z, y).
Axes of the slice: x: 2, y: 2, z: 4, core: 2. Of those that a mesh axis runs over, the one named last changes fastest.
Arguments:
- block_in: bfloat16 [4, 1024, 1024], P('seq', 'band'), may hold values from -6 to 6
- attention_norm_gain: bfloat16 [1024], P(('seq', 'band')), may hold values from 0.5 to 1.5
- attention_norm_bias: bfloat16 [1024], P(('seq', 'band')), may hold values from -3 to 3
- query_key_value: bfloat16 [1024, 3072], P(('seq', 'band')), may hold values from -0.1875 to 0.1875
- query_bias: bfloat16 [1024], P(('seq', 'band')), may hold values from -3 to 3
- value_bias: bfloat16 [1024], P(('seq', 'band')), may hold values from -3 to 3
- output_weight: bfloat16 [1024, 1024], P(('seq', 'band')), may hold values from -1.5 to 1.5
- output_bias: bfloat16 [1024], P(('seq', 'band')), may hold values from -3 to 3
- mlp_norm_gain: bfloat16 [1024], P(('seq', 'band')), may hold values from 0.5 to 1.5
- mlp_norm_bias: bfloat16 [1024], P(('seq', 'band')), may hold values from -3 to 3
- mlp_in_weight: bfloat16 [1024, 4096], P(('seq', 'band')), may hold values from -0.1875 to 0.1875
- mlp_in_bias: bfloat16 [4096], P(('seq', 'band')), may hold values from -3 to 3
- mlp_out_weight: bfloat16 [4096, 1024], P(('seq', 'band')), may hold values from -0.09375 to 0.09375
- mlp_out_bias: bfloat16 [1024], P(('seq', 'band')), may hold values from -3 to 3
- cotangent: bfloat16 [4, 1024, 1024], P('seq', 'band'), may hold values from -6 to 6
- segment_ids: int32 [4, 1024], P('seq', 'band'), may hold values from 0 to 7, as said below
- sub_lengths: int32 [4, 8], P('seq'), may hold values from 1 to 640, as said below
Outputs:
- block_out: bfloat16 [4, 1024, 1024], P('seq', 'band')
- input_grad: bfloat16 [4, 1024, 1024], P('seq', 'band')
- grad_attention_norm_gain: float32 [1024], P(('seq', 'band'))
- grad_attention_norm_bias: float32 [1024], P(('seq', 'band'))
- grad_query_key_value: float32 [1024, 3072], P(('seq', 'band'))
- grad_query_bias: float32 [1024], P(('seq', 'band'))
- grad_value_bias: float32 [1024], P(('seq', 'band'))
- grad_output_weight: float32 [1024, 1024], P(('seq', 'band'))
- grad_output_bias: float32 [1024], P(('seq', 'band'))
- grad_mlp_norm_gain: float32 [1024], P(('seq', 'band'))
- grad_mlp_norm_bias: float32 [1024], P(('seq', 'band'))
- grad_mlp_in_weight: float32 [1024, 4096], P(('seq', 'band'))
- grad_mlp_in_bias: float32 [4096], P(('seq', 'band'))
- grad_mlp_out_weight: float32 [4096, 1024], P(('seq', 'band'))
- grad_mlp_out_bias: float32 [1024], P(('seq', 'band'))
Inputs may be any that keep to these rules, and one draw needn't show every extreme that they name: `segment_ids`: in each sequence the largest subgrid holds exactly 640 slots; the slots of a subgrid may lie anywhere in the sequence. `sub_lengths`: each length is at most the number of slots of its subgrid, and the largest subgrid of each sequence has length 640.
All inputs are finite; a program needn't handle non-finite values.
Results may differ from a plain program's by a relative error of at most 0.012.
Values may be sent and summed in bfloat16 or wider, within the bound.
A program may use at most 256 MiB of HBM per device.

v0:
```python
import math

import jax
import jax.numpy as jnp
from jax import lax
from jax.sharding import PartitionSpec as P

D = 1024
HEADS = 16
HEAD_DIM = 64
SUBGRIDS = 8


EPSILON = 1e-05
NEGATIVE = -1e30


def prefix(part, axis, combine, identity):
    place = lax.axis_index(axis)
    gathered = lax.all_gather(part, axis)
    state = jnp.zeros_like(part) + jnp.asarray(identity, part.dtype)

    def one(lap, state):
        return combine(state, lax.dynamic_index_in_dim(gathered, lap, 0, False))

    return lax.fori_loop(0, place, one, state)


def layer_norm(values_in, norm_gain, norm_shift):
    average = jnp.mean(values_in, axis=-1, keepdims=True)
    centered = values_in - average
    variance = jnp.mean(centered * centered, axis=-1, keepdims=True)
    return centered * lax.rsqrt(variance + EPSILON) * norm_gain + norm_shift


def gelu_exact(values_in):
    return jax.nn.gelu(values_in, approximate=False)


def add_counts(first_part, second_part):
    return first_part + second_part


def block_scores(query_part, key_part, seg_part, code_part, scale_factor):
    scores = (
        jnp.einsum("qhe,khe->hqk", query_part, key_part, preferred_element_type=jnp.float32)
        * scale_factor
    )
    allowed = (seg_part[:, None] == code_part[None, :])[None]
    return (jnp.where(allowed, scores, NEGATIVE), allowed)


def split_blocks(array_in, block_rows):
    return array_in.reshape((array_in.shape[0] // block_rows, block_rows) + array_in.shape[1:])


def shards(
    block_in,
    attention_norm_gain,
    attention_norm_bias,
    query_key_value,
    query_bias,
    value_bias,
    output_weight,
    output_bias,
    mlp_norm_gain,
    mlp_norm_bias,
    mlp_in_weight,
    mlp_in_bias,
    mlp_out_weight,
    mlp_out_bias,
    cotangent,
    segment_ids,
    sub_lengths,
):
    float_type = jnp.float32
    half_type = jnp.bfloat16
    rows_local = block_in.shape[1]
    seq_length = rows_local * lax.axis_size("band")
    scale_factor = HEAD_DIM ** (-0.5)
    block_rows = math.gcd(seq_length, 1024)
    seg_local = segment_ids[0]
    labels = jnp.arange(SUBGRIDS, dtype=jnp.int32)
    onehot_ids = (seg_local[:, None] == labels[None, :]).astype(jnp.int32)
    earlier_counts = prefix(
        jnp.sum(onehot_ids, axis=0), "band", add_counts, jnp.zeros((SUBGRIDS,), jnp.int32)
    )
    before = jnp.cumsum(onehot_ids, axis=0) - onehot_ids + earlier_counts[None, :]
    patch_rank = jnp.sum(before * onehot_ids, axis=1)
    limits = jnp.sum(onehot_ids * sub_lengths[0][None, :], axis=1)
    realness = patch_rank < limits
    key_codes = jnp.where(realness, seg_local, -1)
    gathered = (
        lax.all_gather(attention_norm_gain, ("seq", "band"), axis=0, tiled=True),
        lax.all_gather(attention_norm_bias, ("seq", "band"), axis=0, tiled=True),
        lax.all_gather(query_key_value, ("seq", "band"), axis=0, tiled=True),
        lax.all_gather(query_bias, ("seq", "band"), axis=0, tiled=True),
        lax.all_gather(value_bias, ("seq", "band"), axis=0, tiled=True),
        lax.all_gather(output_weight, ("seq", "band"), axis=0, tiled=True),
        lax.all_gather(output_bias, ("seq", "band"), axis=0, tiled=True),
        lax.all_gather(mlp_norm_gain, ("seq", "band"), axis=0, tiled=True),
        lax.all_gather(mlp_norm_bias, ("seq", "band"), axis=0, tiled=True),
        lax.all_gather(mlp_in_weight, ("seq", "band"), axis=0, tiled=True),
        lax.all_gather(mlp_in_bias, ("seq", "band"), axis=0, tiled=True),
        lax.all_gather(mlp_out_weight, ("seq", "band"), axis=0, tiled=True),
        lax.all_gather(mlp_out_bias, ("seq", "band"), axis=0, tiled=True),
    )
    (
        gain_one,
        shift_one,
        joint_weight,
        bias_query,
        bias_value,
        proj_weight,
        proj_bias,
        gain_two,
        shift_two,
        up_weight,
        up_bias,
        down_weight,
        down_bias,
    ) = gathered
    inputs = block_in[0].astype(float_type)
    normed_float, norm_pull_one = jax.vjp(
        layer_norm, inputs, gain_one.astype(float_type), shift_one.astype(float_type)
    )
    normed_one = normed_float.astype(half_type)
    mixed_all = jnp.dot(normed_one, joint_weight, preferred_element_type=float_type)
    queries = (mixed_all[:, :D] + bias_query.astype(float_type)).astype(half_type)
    keys_local = mixed_all[:, D : 2 * D].astype(half_type)
    values_local = (mixed_all[:, 2 * D :] + bias_value.astype(float_type)).astype(half_type)
    keys_seq, values_seq, codes_seq = (
        lax.all_gather(keys_local, "band", axis=0, tiled=True),
        lax.all_gather(values_local, "band", axis=0, tiled=True),
        lax.all_gather(key_codes, "band", axis=0, tiled=True),
    )
    query_heads = queries.reshape(rows_local, HEADS, HEAD_DIM)
    key_blocks = split_blocks(keys_seq.reshape(seq_length, HEADS, HEAD_DIM), block_rows)
    value_blocks = split_blocks(values_seq.reshape(seq_length, HEADS, HEAD_DIM), block_rows)
    code_blocks = split_blocks(codes_seq, block_rows)

    def stats_step(running, block_items):
        top_now, total_now = running
        key_part, code_part = block_items
        scores, allowed = block_scores(query_heads, key_part, seg_local, code_part, scale_factor)
        top_new = jnp.maximum(top_now, jnp.max(scores, axis=-1))
        exp_terms = jnp.where(allowed, jnp.exp(scores - top_new[..., None]), 0.0)
        return (
            (top_new, total_now * jnp.exp(top_now - top_new) + jnp.sum(exp_terms, axis=-1)),
            None,
        )

    start_stats = (
        jnp.full((HEADS, rows_local), NEGATIVE, float_type),
        jnp.zeros((HEADS, rows_local), float_type),
    )
    (top_final, total_final), unused_stats = lax.scan(
        stats_step, start_stats, (key_blocks, code_blocks)
    )
    log_total = top_final + jnp.log(total_final)

    def value_step(accum_out, block_items):
        key_part, value_part, code_part = block_items
        scores, allowed = block_scores(query_heads, key_part, seg_local, code_part, scale_factor)
        soft_probs = jnp.where(allowed, jnp.exp(scores - log_total[..., None]), 0.0).astype(
            half_type
        )
        return (
            accum_out
            + jnp.einsum("hqk,khe->qhe", soft_probs, value_part, preferred_element_type=float_type),
            None,
        )

    attended, unused_values = lax.scan(
        value_step,
        jnp.zeros((rows_local, HEADS, HEAD_DIM), float_type),
        (key_blocks, value_blocks, code_blocks),
    )
    attended_low = attended.reshape(rows_local, D).astype(half_type)
    residual = (
        inputs
        + jnp.dot(attended_low, proj_weight, preferred_element_type=float_type)
        + proj_bias.astype(float_type)
    )
    normed_float_two, norm_pull_two = jax.vjp(
        layer_norm, residual, gain_two.astype(float_type), shift_two.astype(float_type)
    )
    normed_two = normed_float_two.astype(half_type)
    hidden_pre = jnp.dot(normed_two, up_weight, preferred_element_type=float_type) + up_bias.astype(
        float_type
    )
    hidden_value, gelu_pull = jax.vjp(gelu_exact, hidden_pre)
    hidden_act = hidden_value.astype(half_type)
    block_result = (
        residual
        + jnp.dot(hidden_act, down_weight, preferred_element_type=float_type)
        + down_bias.astype(float_type)
    )
    gathered_back = (
        lax.all_gather(attention_norm_gain, ("seq", "band"), axis=0, tiled=True),
        lax.all_gather(attention_norm_bias, ("seq", "band"), axis=0, tiled=True),
        lax.all_gather(query_key_value, ("seq", "band"), axis=0, tiled=True),
        lax.all_gather(query_bias, ("seq", "band"), axis=0, tiled=True),
        lax.all_gather(value_bias, ("seq", "band"), axis=0, tiled=True),
        lax.all_gather(output_weight, ("seq", "band"), axis=0, tiled=True),
        lax.all_gather(output_bias, ("seq", "band"), axis=0, tiled=True),
        lax.all_gather(mlp_norm_gain, ("seq", "band"), axis=0, tiled=True),
        lax.all_gather(mlp_norm_bias, ("seq", "band"), axis=0, tiled=True),
        lax.all_gather(mlp_in_weight, ("seq", "band"), axis=0, tiled=True),
        lax.all_gather(mlp_in_bias, ("seq", "band"), axis=0, tiled=True),
        lax.all_gather(mlp_out_weight, ("seq", "band"), axis=0, tiled=True),
        lax.all_gather(mlp_out_bias, ("seq", "band"), axis=0, tiled=True),
    )
    joint_back = gathered_back[2]
    proj_back = gathered_back[5]
    up_back = gathered_back[9]
    down_back = gathered_back[11]
    grad_out = cotangent[0].astype(float_type) * realness[:, None].astype(float_type)
    grad_mlp = grad_out.astype(half_type)
    grad_down_weight = jnp.einsum(
        "rf,rd->fd", hidden_act, grad_mlp, preferred_element_type=float_type
    )
    grad_down_bias = jnp.sum(grad_mlp.astype(float_type), axis=0)
    grad_act = jnp.einsum("rd,fd->rf", grad_mlp, down_back, preferred_element_type=float_type)
    grad_pre = gelu_pull(grad_act)[0].astype(half_type)
    grad_up_weight = jnp.einsum(
        "rd,rf->df", normed_two, grad_pre, preferred_element_type=float_type
    )
    grad_up_bias = jnp.sum(grad_pre.astype(float_type), axis=0)
    grad_normed_two = jnp.einsum("rf,df->rd", grad_pre, up_back, preferred_element_type=float_type)
    grad_resid_part, grad_gain_two, grad_shift_two = norm_pull_two(grad_normed_two)
    grad_residual = grad_out + grad_resid_part
    grad_branch = grad_residual.astype(half_type)
    grad_proj_weight = jnp.einsum(
        "rd,re->de", attended_low, grad_branch, preferred_element_type=float_type
    )
    grad_proj_bias = jnp.sum(grad_branch.astype(float_type), axis=0)
    grad_attended = jnp.einsum(
        "re,de->rd", grad_branch, proj_back, preferred_element_type=float_type
    ).astype(half_type)
    grad_heads = grad_attended.reshape(rows_local, HEADS, HEAD_DIM)
    row_delta = jnp.sum(grad_heads.astype(float_type) * attended, axis=-1).T
    keys_back = lax.all_gather(keys_local, "band", axis=0, tiled=True)
    values_back = lax.all_gather(values_local, "band", axis=0, tiled=True)
    codes_back = lax.all_gather(key_codes, "band", axis=0, tiled=True)
    key_back_blocks = split_blocks(keys_back.reshape(seq_length, HEADS, HEAD_DIM), block_rows)
    value_back_blocks = split_blocks(values_back.reshape(seq_length, HEADS, HEAD_DIM), block_rows)
    code_back_blocks = split_blocks(codes_back, block_rows)

    def key_step(query_accum, block_items):
        key_part, value_part, code_part = block_items
        scores, allowed = block_scores(query_heads, key_part, seg_local, code_part, scale_factor)
        soft_probs = jnp.where(allowed, jnp.exp(scores - log_total[..., None]), 0.0)
        grad_probs = jnp.einsum(
            "qhe,khe->hqk", grad_heads, value_part, preferred_element_type=float_type
        )
        grad_scores = (soft_probs * (grad_probs - row_delta[..., None])).astype(half_type)
        query_accum = query_accum + jnp.einsum(
            "hqk,khe->qhe", grad_scores, key_part, preferred_element_type=float_type
        )
        return (query_accum, None)

    query_total, joined_blocks = lax.scan(
        key_step,
        jnp.zeros((rows_local, HEADS, HEAD_DIM), float_type),
        (key_back_blocks, value_back_blocks, code_back_blocks),
    )
    grad_query = (query_total * scale_factor).reshape(rows_local, D)
    query_seq = lax.all_gather(queries, "band", axis=0, tiled=True)
    grad_seq = lax.all_gather(grad_attended, "band", axis=0, tiled=True)
    total_seq = lax.all_gather(log_total, "band", axis=1, tiled=True)
    delta_seq = lax.all_gather(row_delta, "band", axis=1, tiled=True)
    seg_seq = lax.all_gather(seg_local, "band", axis=0, tiled=True)
    block_count = seq_length // block_rows
    key_heads_local = keys_local.reshape(rows_local, HEADS, HEAD_DIM)
    value_heads_local = values_local.reshape(rows_local, HEADS, HEAD_DIM)

    def query_step(running, block_items):
        key_accum, value_accum = running
        query_part, grad_part, total_part, delta_part, seg_part = block_items
        scores, allowed = block_scores(
            query_part, key_heads_local, seg_part, key_codes, scale_factor
        )
        soft_probs = jnp.where(allowed, jnp.exp(scores - total_part[..., None]), 0.0)
        grad_probs = jnp.einsum(
            "qhe,khe->hqk", grad_part, value_heads_local, preferred_element_type=float_type
        )
        grad_scores = (soft_probs * (grad_probs - delta_part[..., None])).astype(half_type)
        key_accum = key_accum + jnp.einsum(
            "hqk,qhe->khe", grad_scores, query_part, preferred_element_type=float_type
        )
        value_accum = value_accum + jnp.einsum(
            "hqk,qhe->khe",
            soft_probs.astype(half_type),
            grad_part,
            preferred_element_type=float_type,
        )
        return ((key_accum, value_accum), None)

    zero_heads = jnp.zeros((rows_local, HEADS, HEAD_DIM), float_type)
    (key_total, value_total), query_blocks = lax.scan(
        query_step,
        (zero_heads, zero_heads),
        (
            split_blocks(query_seq.reshape(seq_length, HEADS, HEAD_DIM), block_rows),
            split_blocks(grad_seq.reshape(seq_length, HEADS, HEAD_DIM), block_rows),
            total_seq.reshape(HEADS, block_count, block_rows).transpose(1, 0, 2),
            delta_seq.reshape(HEADS, block_count, block_rows).transpose(1, 0, 2),
            split_blocks(seg_seq, block_rows),
        ),
    )
    grad_key = (key_total * scale_factor).reshape(rows_local, D)
    grad_value = value_total.reshape(rows_local, D)
    grad_query_low = grad_query.astype(half_type)
    grad_value_low = grad_value.astype(half_type)
    grad_mixed = jnp.concatenate(
        [grad_query_low, grad_key.astype(half_type), grad_value_low], axis=1
    )
    grad_joint_weight = jnp.einsum(
        "rd,rm->dm", normed_one, grad_mixed, preferred_element_type=float_type
    )
    grad_bias_query = jnp.sum(grad_query_low.astype(float_type), axis=0)
    grad_bias_value = jnp.sum(grad_value_low.astype(float_type), axis=0)
    grad_normed_one = jnp.einsum(
        "rm,dm->rd", grad_mixed, joint_back, preferred_element_type=float_type
    )
    grad_input_part, grad_gain_one, grad_shift_one = norm_pull_one(grad_normed_one)
    input_grad = (grad_residual + grad_input_part).astype(half_type)
    shard_grads = (
        lax.psum_scatter(grad_gain_one, ("seq", "band"), scatter_dimension=0, tiled=True),
        lax.psum_scatter(grad_shift_one, ("seq", "band"), scatter_dimension=0, tiled=True),
        lax.psum_scatter(grad_joint_weight, ("seq", "band"), scatter_dimension=0, tiled=True),
        lax.psum_scatter(grad_bias_query, ("seq", "band"), scatter_dimension=0, tiled=True),
        lax.psum_scatter(grad_bias_value, ("seq", "band"), scatter_dimension=0, tiled=True),
        lax.psum_scatter(grad_proj_weight, ("seq", "band"), scatter_dimension=0, tiled=True),
        lax.psum_scatter(grad_proj_bias, ("seq", "band"), scatter_dimension=0, tiled=True),
        lax.psum_scatter(grad_gain_two, ("seq", "band"), scatter_dimension=0, tiled=True),
        lax.psum_scatter(grad_shift_two, ("seq", "band"), scatter_dimension=0, tiled=True),
        lax.psum_scatter(grad_up_weight, ("seq", "band"), scatter_dimension=0, tiled=True),
        lax.psum_scatter(grad_up_bias, ("seq", "band"), scatter_dimension=0, tiled=True),
        lax.psum_scatter(grad_down_weight, ("seq", "band"), scatter_dimension=0, tiled=True),
        lax.psum_scatter(grad_down_bias, ("seq", "band"), scatter_dimension=0, tiled=True),
    )
    return (
        block_result.astype(half_type)[None],
        input_grad[None],
        shard_grads[0],
        shard_grads[1],
        shard_grads[2],
        shard_grads[3],
        shard_grads[4],
        shard_grads[5],
        shard_grads[6],
        shard_grads[7],
        shard_grads[8],
        shard_grads[9],
        shard_grads[10],
        shard_grads[11],
        shard_grads[12],
    )


def solution(mesh):
    return jax.shard_map(
        shards,
        mesh=mesh,
        in_specs=(
            P("seq", "band", None),
            P(("seq", "band")),
            P(("seq", "band")),
            P(("seq", "band"), None),
            P(("seq", "band")),
            P(("seq", "band")),
            P(("seq", "band"), None),
            P(("seq", "band")),
            P(("seq", "band")),
            P(("seq", "band")),
            P(("seq", "band"), None),
            P(("seq", "band")),
            P(("seq", "band"), None),
            P(("seq", "band")),
            P("seq", "band", None),
            P("seq", "band"),
            P("seq", None),
        ),
        out_specs=(
            P("seq", "band", None),
            P("seq", "band", None),
            P(("seq", "band")),
            P(("seq", "band")),
            P(("seq", "band"), None),
            P(("seq", "band")),
            P(("seq", "band")),
            P(("seq", "band"), None),
            P(("seq", "band")),
            P(("seq", "band")),
            P(("seq", "band")),
            P(("seq", "band"), None),
            P(("seq", "band")),
            P(("seq", "band"), None),
            P(("seq", "band")),
        ),
        check_vma=False,
    )
```

profile of v0, /device:TPU:1, one launch (start us, length us, event | category | flops | bytes accessed | tf_op | source)
XLA Modules:
  0.0 1536.3 jit_solution(15341018853794096763)
XLA Ops:
  14.7 42.1 %all-reduce.19 = (bf16[1024]{0:T(1024)(128)(2,1)S(1)}, bf16[1024]{0:T(1024)(128)(2,1)S(1)}, bf16[1024]{0:T(1024)(128)(2,1)S(1)}, bf16[1024]{0:T(1024)(128)(2,1)S...) all-reduce(bf16[1024]{0:T(1024)(128)(2,1)S(1)} %dynamic-update-slic, ...), channel_id=1, replica_groups=mesh['seq'=4,'band'=8] {'seq','band'}, use_global_device_ids=true, to_apply=%add.1 | all-reduce | flops 8192 | bytes 32768
  59.1 24.3 %all-gather.13.cloned.1.call-done = bf16[1024,3072]{1,0:T(8,128)(2,1)} async-done(((bf16[32,3072]{1,0:T(8,128)(2,1)}), bf16[1024,3072]{1,0:T(8,128)(2,1)}) %all-gather.13.cloned.1.call-update) | async-done | bytes 6291472 | tf_op jit(solution)/shard_map/all_gather | solution.py:96
  83.3 4.0 fusion.83
  92.5 7.8 all-reduce.3
  100.6 60.9 %all-gather.3 = bf16[32,1,128]{2,1,0:T(2,128)(2,1)S(1)} all-gather(bf16[1,1,128]{2,1,0:T(2,128)(2,1)S(1)} %bitcast.154), channel_id=1, replica_groups=mesh['seq'=4,'band'=8] {'seq','band'}, dimensions={0}, use_global_device_ids=true | all-gather | bytes 8448 | tf_op jit(solution)/shard_map/all_gather | solution.py:104
  161.8 18.0 %all-gather.2 = s32[8,1,128]{2,1,0:T(1,128)S(1)} all-gather(s32[1,1,128]{2,1,0:T(1,128)S(1)} %select_bitcast_fusion), channel_id=1, replica_groups=mesh['seq'=4,'band'=8] {'band'}, dimensions={0}, use_global_device_ids=true | all-gather | bytes 4608 | tf_op jit(solution)/shard_map/all_gather | solution.py:135
  192.1 7.2 fusion.91
  199.3 45.5 %all-gather.19.cloned.1.call-done = bf16[1024,1024]{1,0:T(8,128)(2,1)} async-done(((bf16[32,1024]{1,0:T(8,128)(2,1)}), bf16[1024,1024]{1,0:T(8,128)(2,1)}) %all-gather.19.cloned.1.call-update) | async-done | bytes 2097168 | tf_op jit(solution)/shard_map/all_gather | solution.py:99
  247.2 76.7 %all-gather.21.cloned.1.call-done = bf16[1024,4096]{1,0:T(8,128)(2,1)} async-done(((bf16[32,4096]{1,0:T(8,128)(2,1)}), bf16[1024,4096]{1,0:T(8,128)(2,1)}) %all-gather.21.cloned.1.call-update) | async-done | bytes 8388624 | tf_op jit(solution)/shard_map/all_gather | solution.py:103
  323.9 9.6 multiply_convert_fusion.4
  333.6 69.2 %all-gather.23.cloned.1.call-done = bf16[4096,1024]{1,0:T(8,128)(2,1)} async-done(((bf16[128,1024]{1,0:T(8,128)(2,1)}), bf16[4096,1024]{1,0:T(8,128)(2,1)}) %all-gather.23.cloned.1.call-update) | async-done | bytes 8388624 | tf_op jit(solution)/shard_map/all_gather | solution.py:105
  402.8 8.7 convert_reduce_fusion
  419.5 3.8 fusion.94
  423.4 15.5 %all-gather.1 = s32[1,1024]{1,0:T(1,128)S(1)} all-gather(s32[1,128]{1,0:T(1,128)} %param.34), channel_id=3, replica_groups=mesh['seq'=4,'band'=8] {'band'}, dimensions={1}, use_global_device_ids=true | all-gather | bytes 4608 | tf_op jit(solution)/shard_map/all_gather | solution.py:273
  444.0 8.0 all-gather.25.cloned.1.call-done
  452.0 3.9 copy.53
  456.0 26.4 %all_gather.96 = f32[16,1024]{1,0:T(8,128)} all-gather(f32[16,128]{1,0:T(8,128)} %copy-done.17), channel_id=1, replica_groups=mesh['seq'=4,'band'=8] {'band'}, dimensions={1}, use_global_device_ids=true | all-gather | bytes 73728 | tf_op jit(solution)/shard_map/all_gather | solution.py:271
  482.4 6.2 fusion.93
  492.1 27.0 %all_gather.98 = f32[16,1024]{1,0:T(8,128)} all-gather(f32[16,128]{1,0:T(8,128)S(1)} %bitcast.144), channel_id=1, replica_groups=mesh['seq'=4,'band'=8] {'band'}, dimensions={1}, use_global_device_ids=true | all-gather | bytes 73728 | tf_op jit(solution)/shard_map/all_gather | solution.py:272
  519.1 10.1 convert_reduce_fusion.5
  529.2 4.0 copy.55
  533.1 6.9 convert_reduce_fusion.4
  540.0 9.6 fusion.32
  549.6 7.6 fusion.53
  557.8 8.2 fusion.86
  567.0 8.1 fusion.76
  575.9 5.5 fusion.36
  581.5 5.1 fusion.87
  587.0 52.2 %all-reduce.18 = (f32[1024]{0:T(1024)S(1)}, f32[1024]{0:T(1024)S(1)}, f32[1024]{0:T(1024)S(1)}, f32[1024]{0:T(1024)S(1)}, f32[1024]{0:T(1024)S(1)}, /*index=5*/f...) all-reduce(f32[1024]{0:T(1024)S(1)} %get-tuple-element.138, ...), channel_id=4, replica_groups=mesh['seq'=4,'band'=8] {'seq','band'}, use_global_device_ids=true, to_apply=%region_18.19.clone | all-reduce | flops 12288 | bytes 98304
  645.5 162.4 %reduce-scatter.5.cloned.1.call-done = f32[32,3072]{1,0:T(8,128)} async-done(((f32[1024,3072]{1,0:T(8,128)}), f32[32,3072]{1,0:T(8,128)}) %reduce-scatter.5.cloned.1.call-update) | async-done | bytes 393232 | tf_op jit(solution)/shard_map/reduce_scatter | solution.py:332
  807.9 361.1 %reduce-scatter.9.cloned.1.call-done = f32[32,4096]{1,0:T(8,128)} async-done(((f32[1024,4096]{1,0:T(8,128)}), f32[32,4096]{1,0:T(8,128)}) %reduce-scatter.9.cloned.1.call-update) | async-done | bytes 524304 | tf_op jit(solution)/shard_map/reduce_scatter | solution.py:339
  1169.0 360.2 %reduce-scatter.11.cloned.1.call-done = f32[128,1024]{1,0:T(8,128)} async-done(((f32[4096,1024]{1,0:T(8,128)}), f32[128,1024]{1,0:T(8,128)}) %reduce-scatter.11.cloned.1.call-update) | async-done | bytes 524304 | tf_op jit(solution)/shard_map/reduce_scatter | solution.py:341
  (204 shorter events, 54.7 us)
Async XLA Ops:
  7.2 76.2 %all-gather.13.cloned.1.call-start = ((), (), s32[]{:S(2)}) async-start(), calls=%async_computation.4 | async-start | bytes 6488064 | tf_op jit(solution)/shard_map/all_gather | solution.py:96
  7.9 173.5 %all-gather.17.cloned.1.call-start = ((), (), s32[]{:S(2)}) async-start(), calls=%async_computation.6 | async-start | bytes 2359296 | tf_op jit(solution)/shard_map/all_gather | solution.py:133
  57.9 29.5 %copy-start.18 = (f32[128]{0:T(128)}, f32[128]{0:T(128)S(1)}, u32[]{:S(2)}) copy-start(f32[128]{0:T(128)S(1)} %broadcast_multiply_fusion.1) | copy-start | bytes 1540
  59.0 28.3 %copy-start.43 = (f32[128]{0:T(128)}, f32[128]{0:T(128)S(1)}, u32[]{:S(2)}) copy-start(f32[128]{0:T(128)S(1)} %fusion.47) | copy-start | bytes 1540
  59.1 28.3 %copy-start.21 = (f32[128]{0:T(128)}, f32[128]{0:T(128)S(1)}, u32[]{:S(2)}) copy-start(f32[128]{0:T(128)S(1)} %fusion.60) | copy-start | bytes 1540
  87.4 13.2 copy-start.45
  87.4 74.2 %copy-start.42 = (s32[1,8]{1,0:T(1,128)S(1)}, s32[1,8]{1,0:T(1,128)}, u32[]{:S(2)}) copy-start(s32[1,8]{1,0:T(1,128)} %param.35) | copy-start | bytes 100
  88.2 101.0 %all-gather.15.cloned.1.call-start = ((), (), s32[]{:S(2)}) async-start(), calls=%async_computation.5 | async-start | bytes 2359296 | tf_op jit(solution)/shard_map/all_gather | solution.py:134
  89.1 91.7 %copy-start.9 = (bf16[128,1024]{1,0:T(8,128)(2,1)}, bf16[128,1024]{1,0:T(8,128)(2,1)S(1)}, u32[]{:S(2)}) copy-start(bf16[128,1024]{1,0:T(8,128)(2,1)S(1)} %get-tuple-element.187) | copy-start | bytes 786436
  89.1 155.7 %all-gather.19.cloned.1.call-start = ((), (), s32[]{:S(2)}) async-start(), calls=%async_computation.7 | async-start | bytes 2162688 | tf_op jit(solution)/shard_map/all_gather | solution.py:99
  89.7 234.2 %all-gather.21.cloned.1.call-start = ((), (), s32[]{:S(2)}) async-start(), calls=%async_computation.8 | async-start | bytes 8650752 | tf_op jit(solution)/shard_map/all_gather | solution.py:103
  90.2 312.5 %all-gather.23.cloned.1.call-start = ((), (), s32[]{:S(2)}) async-start(), calls=%async_computation.9 | async-start | bytes 8650752 | tf_op jit(solution)/shard_map/all_gather | solution.py:105
  90.8 361.2 %all-gather.25.cloned.1.call-start = ((), (), s32[]{:S(2)}) async-start(), calls=%async_computation.10 | async-start | bytes 2359296 | tf_op jit(solution)/shard_map/all_gather | solution.py:269
  161.8 19.5 %copy-start.34 = (s32[128]{0:T(128)}, s32[128]{0:T(128)S(1)}, u32[]{:S(2)}) copy-start(s32[128]{0:T(128)S(1)} %get-tuple-element.143) | copy-start | bytes 1540
  161.8 19.5 %copy-start.35 = (s32[128]{0:T(128)}, s32[128]{0:T(128)S(1)}, u32[]{:S(2)}) copy-start(s32[128]{0:T(128)S(1)} %get-tuple-element.144) | copy-start | bytes 1540
  180.8 348.4 %all-gather.27.cloned.1.call-start = ((), (), s32[]{:S(2)}) async-start(), calls=%async_computation.11 | async-start | bytes 2359296 | tf_op jit(solution)/shard_map/all_gather | solution.py:270
  192.1 7.2 copy-start.10
  192.1 52.7 %copy-start.1 = (bf16[1,128,1024]{2,1,0:T(8,128)(2,1)S(1)}, bf16[1,128,1024]{2,1,0:T(8,128)(2,1)}, u32[]{:S(2)}) copy-start(bf16[1,128,1024]{2,1,0:T(8,128)(2,1)} %param.19) | copy-start | bytes 786436
  199.3 134.3 %copy-start.11 = (bf16[128,16,64]{0,2,1:T(8,128)(2,1)}, bf16[128,16,64]{0,2,1:T(8,128)(2,1)S(1)}, u32[]{:S(2)}) copy-start(bf16[128,16,64]{0,2,1:T(8,128)(2,1)S(1)} %get-tuple-element.192) | copy-start | bytes 786436
  246.9 164.6 %copy-start.28 = (f32[128]{0:T(128)}, f32[128]{0:T(128)S(1)}, u32[]{:S(2)}) copy-start(f32[128]{0:T(128)S(1)} %broadcast_multiply_fusion) | copy-start | bytes 1540
  247.2 164.4 %copy-start.30 = (f32[128]{0:T(128)}, f32[128]{0:T(128)S(1)}, u32[]{:S(2)}) copy-start(f32[128]{0:T(128)S(1)} %fusion.61) | copy-start | bytes 1540
  323.9 78.9 %copy-start.5 = (bf16[1,128,1024]{2,1,0:T(8,128)(2,1)S(1)}, bf16[1,128,1024]{2,1,0:T(8,128)(2,1)}, u32[]{:S(2)}) copy-start(bf16[1,128,1024]{2,1,0:T(8,128)(2,1)} %param.33) | copy-start | bytes 786436
  323.9 78.9 %copy-start.36 = (f32[128]{0:T(128)S(1)}, f32[128]{0:T(128)}, u32[]{:S(2)}) copy-start(f32[128]{0:T(128)} %compare_convert_fusion) | copy-start | bytes 1540
  402.8 8.8 copy-start.3
  419.4 226.1 %reduce-scatter.7.cloned.1.call-start = ((), (), s32[]{:S(2)}) async-start(), calls=%async_computation.13 | async-start | bytes 4325376 | tf_op jit(solution)/shard_map/reduce_scatter | solution.py:335
  423.3 384.6 %reduce-scatter.5.cloned.1.call-start = ((), (), s32[]{:S(2)}) async-start(), calls=%async_computation.12 | async-start | bytes 12976128 | tf_op jit(solution)/shard_map/reduce_scatter | solution.py:332
  557.2 611.8 %reduce-scatter.9.cloned.1.call-start = ((), (), s32[]{:S(2)}) async-start(), calls=%async_computation.14 | async-start | bytes 17301504 | tf_op jit(solution)/shard_map/reduce_scatter | solution.py:339
  566.0 963.1 %reduce-scatter.11.cloned.1.call-start = ((), (), s32[]{:S(2)}) async-start(), calls=%async_computation.15 | async-start | bytes 17301504 | tf_op jit(solution)/shard_map/reduce_scatter | solution.py:341
  575.9 5.5 copy-start.13
  575.9 5.5 copy-start.14
  575.9 5.5 copy-start.19
  581.5 63.0 %copy-start.41 = (f32[128]{0:T(128)S(1)}, f32[128]{0:T(128)}, u32[]{:S(2)}) copy-start(f32[128]{0:T(128)} %copy-done.40) | copy-start | bytes 1540
  (27 other events, 88.1 us)
Sparse Core Ops, SparseCore 0:
  10.9 72.3 all-gather.12
  88.3 46.4 all-gather.16
  137.5 47.8 all-gather.14
  188.2 56.5 all-gather.18
  247.6 76.2 all-gather.20
  326.7 75.9 all-gather.22
  405.5 46.5 all-gather.24
  454.7 48.1 all-gather.26
  505.8 136.7 reduce-scatter.6
  649.0 158.9 reduce-scatter.4
  810.9 358.0 reduce-scatter.8
  1171.8 357.3 reduce-scatter.10
where the time goes:
time: 1540 us
  waiting for transfers between devices  1110 us (72%)
  blocking collectives  250 us (16%)
  matrix products  109 us (7%)
  local copies, waits for them, and re-layouts  36.9 us (2%)
  between operations  15.8 us (1%)
    reduce_scatter x1, waiting for transfers between devices, shards(): lax.psum_scatter(grad_up_weight, ('seq', 'band'), scatter_dimension=0, ti...  361 us
    reduce_scatter x1, waiting for transfers between devices, shards(): lax.psum_scatter(grad_down_weight, ('seq', 'band'), scatter_dimension=0,...  360 us
    reduce_scatter x1, waiting for transfers between devices, shards(): lax.psum_scatter(grad_joint_weight, ('seq', 'band'), scatter_dimension=0,...  162 us
    unnamed x3, blocking collectives  102 us
    all_gather x1, waiting for transfers between devices, shards(): lax.all_gather(mlp_in_weight, ('seq', 'band'), axis=0, tiled=True)  76.7 us
    all_gather x1, waiting for transfers between devices, shards(): lax.all_gather(mlp_out_weight, ('seq', 'band'), axis=0, tiled=True)  69.2 us
    all_gather x1, blocking collectives, shards(): lax.all_gather(mlp_in_bias, ('seq', 'band'), axis=0, tiled=True)  60.9 us
    all_gather x1, waiting for transfers between devices, shards(): lax.all_gather(output_weight, ('seq', 'band'), axis=0, tiled=True)  45.5 us
  transfers between devices with their start and end apart: 12, of which 8 were waited for; matrix products, arithmetic and copies ran while one was open for 10% of the time, Pallas kernels for 0%

commit v1 on v0

--- a/solution.py
+++ b/solution.py
@@ -1,8 +1,11 @@
+import functools
 import math
 
 import jax
 import jax.numpy as jnp
 from jax import lax
+from jax.experimental import pallas as pl
+from jax.experimental.pallas import tpu as pltpu
 from jax.sharding import PartitionSpec as P
 
 D = 1024
@@ -85,7 +88,14 @@
     earlier_counts = prefix(
         jnp.sum(onehot_ids, axis=0), "band", add_counts, jnp.zeros((SUBGRIDS,), jnp.int32)
     )
-    before = jnp.cumsum(onehot_ids, axis=0) - onehot_ids + earlier_counts[None, :]
+    slots = jnp.arange(rows_local)
+    earlier = (slots[None, :] < slots[:, None]).astype(float_type)
+    before = (
+        jnp.dot(earlier, onehot_ids.astype(float_type), precision=lax.Precision.HIGHEST).astype(
+            jnp.int32
+        )
+        + earlier_counts[None, :]
+    )
     patch_rank = jnp.sum(before * onehot_ids, axis=1)
     limits = jnp.sum(onehot_ids * sub_lengths[0][None, :], axis=1)
     realness = patch_rank < limits
@@ -360,9 +370,903 @@
     )
 
 
+F32 = jnp.float32
+BF16 = jnp.bfloat16
+MESH_ID = pl.DeviceIdType.MESH
+ROWS = 128
+LANES = 128
+
+
+def dot(lhs, rhs):
+    return jnp.dot(lhs, rhs, preferred_element_type=F32)
+
+
+def dot_nt(lhs, rhs):
+    return lax.dot_general(lhs, rhs, (((1,), (1,)), ((), ())), preferred_element_type=F32)
+
+
+def dot_tn(lhs, rhs):
+    return lax.dot_general(lhs, rhs, (((0,), (0,)), ((), ())), preferred_element_type=F32)
+
+
+def fused_kernel(copies, *refs):
+    (
+        xin, cin, sgin, pkin, wq, wo, wi, wd,
+        out_block, out_input, out_q, out_o, out_i, out_d, out_small,
+        X, N1, N2, GM, GB, SG, SP, FULL, PV,
+        WSQ, RQ, WQ, WO, WSI, RI, WI, WD,
+        QS, KK, VV, QT, KT, VT, CODE, SC, PT, INV, OT, OL,
+        PA, CS, PB, CSB, SB, RV, XO, N2F, HAT, HA, GP,
+        DK, DV, DQ, GMX,
+        GQ, GI, GD, XQ, XI, XD, HQ, HI, HD, ZQ, ZI, ZD, TQ, TI, RGQ, RGI,
+        GO, GOF, XGO, TGO, RGO,
+        VG, VR, SL, SLR, RS_, BG,
+        ssem, rsem,
+    ) = refs
+    s = lax.axis_index("seq")
+    b = lax.axis_index("band")
+    x, c = lax.div(s, 2), lax.rem(s, 2)
+    zh, l = lax.div(b, 4), lax.rem(b, 4)
+    zl, y = lax.div(l, 2), lax.rem(l, 2)
+    t, j = x * 2 + zh, c * 4 + l
+
+    def flip(v, d):
+        return 1 - v if d else v
+
+    def flip_l(d):
+        return flip(zl, d // 2) * 2 + flip(y, d % 2)
+
+    def dev(dx=0, dc=0, dzh=0, dl=0):
+        return (flip(x, dx) * 2 + flip(c, dc), flip(zh, dzh) * 4 + flip_l(dl))
+
+    counter = [0]
+    pending = []
+
+    def slots(n=1):
+        first = counter[0]
+        counter[0] += n
+        assert counter[0] <= copies
+        return first
+
+    def send(src, dst, device, sem):
+        copy = pltpu.make_async_remote_copy(
+            src_ref=src, dst_ref=dst, send_sem=ssem.at[sem], recv_sem=rsem.at[sem],
+            device_id=device, device_id_type=MESH_ID)
+        copy.start()
+        return copy
+
+    def push(src, dst, device, sem):
+        copy = send(src, dst, device, sem)
+        pending.append(copy)
+        return copy
+
+    def arrive(dst, sem):
+        pltpu.make_async_remote_copy(
+            src_ref=dst, dst_ref=dst, send_sem=ssem.at[sem], recv_sem=rsem.at[sem],
+            device_id=dev(dc=1), device_id_type=MESH_ID).wait_recv()
+
+    def left(src, sem):
+        pltpu.make_async_remote_copy(
+            src_ref=src, dst_ref=src, send_sem=ssem.at[sem], recv_sem=rsem.at[sem],
+            device_id=dev(dc=1), device_id_type=MESH_ID).wait_send()
+
+    group_masks = [(dc, dl) for dl in (1, 2, 3, 0) for dc in (0, 1) if (dc, dl) != (0, 0)]
+    line_masks = [(dx, dc, dzh) for dx in (0, 1) for dc in (0, 1) for dzh in (0, 1) if dx + dc + dzh]
+
+    barrier = pltpu.get_barrier_semaphore()
+    peers = [dict(dc=dc, dl=dl) for dc, dl in group_masks]
+    peers += [dict(dx=a, dc=e, dzh=f) for a, e, f in line_masks if (a, e, f) != (0, 1, 0)]
+    for peer in peers:
+        pl.semaphore_signal(barrier, inc=1, device_id=dev(**peer), device_id_type=MESH_ID)
+    pl.semaphore_wait(barrier, len(peers))
+
+    native = c == zh
+    partner = dev(dc=1, dzh=1)
+    their_block = (1 - c) * 4 + l
+
+    sem_px, sem_pc, sem_ps = slots(), slots(), slots()
+
+    @pl.when(native)
+    def _():
+        X[j] = xin[...]
+        SG[j] = sgin[...]
+
+    @pl.when(jnp.logical_not(native))
+    def _():
+        send(sgin, SG.at[their_block], partner, sem_ps)
+        send(xin, X.at[their_block], partner, sem_px)
+
+    sem_s1 = slots(4)
+    for dl in (1, 2, 3):
+        push(pkin, SP.at[dl], dev(dl=dl), sem_s1 + dl)
+
+    for jj in range(8):
+        for ch in range(3):
+            WSQ[jj, ch] = wq[:, ch * D + jj * LANES : ch * D + (jj + 1) * LANES]
+    sem_wq = slots(8)
+    for dc, dl in group_masks:
+        peer_j = flip(c, dc) * 4 + flip_l(dl)
+        push(WSQ.at[peer_j], RQ.at[t, j], dev(dc=dc, dl=dl), sem_wq + dc * 4 + dl)
+    RQ[t, j] = WSQ[j]
+
+    class Gather:
+        def __init__(self, buf):
+            self.buf, self.far, self.near = buf, slots(4), slots(4)
+
+        def start(self):
+            for dl in (1, 2, 3):
+                push(self.buf.at[j], self.buf.at[j], dev(dl=dl), self.far + dl)
+            push(self.buf.at[j], self.buf.at[j], dev(dc=1), self.near)
+
+        def forward(self, dl):
+            block = self.buf.at[c * 4 + flip_l(dl)]
+            arrive(block, self.far + dl)
+            push(block, block, dev(dc=1), self.near + dl)
+
+        def sibling(self, dl):
+            arrive(self.buf.at[(1 - c) * 4 + flip_l(dl)], self.near + dl)
+
+    @pl.when(jnp.logical_not(native))
+    def _():
+        arrive(SG.at[j], sem_ps)
+
+    sem_sg = slots(8)
+    for dc, dl in group_masks:
+        push(SG.at[j], SG.at[j], dev(dc=dc, dl=dl), sem_sg + dc * 4 + dl)
+
+    @pl.when(jnp.logical_not(native))
+    def _():
+        arrive(X.at[j], sem_px)
+
+    gather_x = Gather(X)
+    gather_x.start()
+
+    q_own = x * 4 + c * 2 + zh
+    slab = pkin[...]
+    for dl in (1, 2, 3):
+        arrive(SP.at[dl], sem_s1 + dl)
+        slab += SP[dl]
+    FULL[q_own] = slab
+    sem_s2 = slots(8)
+    for dx, dc, dzh in line_masks:
+        push(FULL.at[q_own], FULL.at[q_own], dev(dx=dx, dc=dc, dzh=dzh), sem_s2 + dx * 4 + dc * 2 + dzh)
+
+    class Spread:
+        def __init__(self, buf):
+            self.buf, self.sem = buf, slots(3)
+
+        def start(self):
+            block = self.buf.at[t]
+            push(block, block, dev(dzh=1), self.sem)
+            push(block, block, dev(dx=1), self.sem + 1)
+
+        def forward(self):
+            block = self.buf.at[x * 2 + 1 - zh]
+            arrive(block, self.sem)
+            push(block, block, dev(dx=1), self.sem + 2)
+
+        def finish(self):
+            arrive(self.buf.at[(1 - x) * 2 + zh], self.sem + 1)
+            arrive(self.buf.at[(1 - x) * 2 + 1 - zh], self.sem + 2)
+
+    for dc, dl in group_masks:
+        arrive(RQ.at[t, flip(c, dc) * 4 + flip_l(dl)], sem_wq + dc * 4 + dl)
+    spread_q = Spread(RQ)
+    spread_q.start()
+
+    for dx, dc, dzh in line_masks:
+        arrive(FULL.at[flip(x, dx) * 4 + flip(c, dc) * 2 + flip(zh, dzh)], sem_s2 + dx * 4 + dc * 2 + dzh)
+    for q in range(8):
+        PV[:, q * LANES : (q + 1) * LANES] = FULL[q]
+    gain1, shift1 = PV[0:1, :], PV[1:2, :]
+
+    def norm_rows(value, gain, shift):
+        average = jnp.mean(value, axis=-1, keepdims=True)
+        centered = value - average
+        root = lax.rsqrt(jnp.mean(centered * centered, axis=-1, keepdims=True) + EPSILON)
+        normal = centered * root
+        return normal, root, normal * gain + shift
+
+    def norm_one(block):
+        def body(i, carry):
+            rows = pl.ds(pl.multiple_of(i * 32, 32), 32)
+            N1[block, rows] = norm_rows(X[block, rows].astype(F32), gain1, shift1)[2].astype(BF16)
+            return carry
+
+        lax.fori_loop(0, ROWS // 32, body, 0)
+
+    norm_one(j)
+    for dl in (1, 2):
+        gather_x.forward(dl)
+    gather_x.sibling(0)
+    norm_one((1 - c) * 4 + l)
+    norm_one(c * 4 + flip_l(1))
+    gather_x.forward(3)
+    norm_one(c * 4 + flip_l(2))
+    spread_q.forward()
+
+    @pl.when(native)
+    def _():
+        GM[j] = cin[...]
+
+    @pl.when(jnp.logical_not(native))
+    def _():
+        send(cin, GM.at[their_block], partner, sem_pc)
+
+    sem_wi = slots(8)
+    for jj in range(8):
+        for ch in range(4):
+            flat = (ch // 2) * 16 + (jj // 4) * 8 + (ch % 2) * 4 + jj % 4
+            WSI[jj, ch] = wi[:, flat * LANES : (flat + 1) * LANES]
+    for dc, dl in group_masks:
+        peer_j = flip(c, dc) * 4 + flip_l(dl)
+        push(WSI.at[peer_j], RI.at[t, j], dev(dc=dc, dl=dl), sem_wi + dc * 4 + dl)
+    RI[t, j] = WSI[j]
+    WD[t] = wd[...]
+
+    sem_wo, sem_wt = slots(4), slots(4)
+    pair_l = c * 2 + zh
+    to_self = jnp.logical_and(x == c, l == pair_l)
+    is_root = jnp.logical_and(x == c, zh == y)
+    root_mask = jnp.abs(x - c) * 2 + jnp.abs(zh - y)
+
+    @pl.when(to_self)
+    def _():
+        WO[l] = wo[...]
+
+    @pl.when(jnp.logical_not(to_self))
+    def _():
+        send(wo, WO.at[l], (x * 2 + x, zh * 4 + pair_l), sem_wo + l)
+
+    for dl in (1, 2, 3):
+        gather_x.sibling(dl)
+        norm_one((1 - c) * 4 + flip_l(dl))
+    norm_one(c * 4 + flip_l(3))
+
+    for dc, dl in group_masks:
+        arrive(SG.at[flip(c, dc) * 4 + flip_l(dl)], sem_sg + dc * 4 + dl)
+    lens = SG[j, 1:2, :]
+    row_ids = lax.broadcasted_iota(jnp.int32, (LANES, LANES), 0)
+    lane_ids = lax.broadcasted_iota(jnp.int32, (LANES, LANES), 1)
+    label_row = lane_ids.astype(F32)
+    label_col = row_ids.astype(F32)
+    earlier = (lane_ids < row_ids).astype(BF16)
+    running = jnp.zeros((1, LANES), F32)
+    for blk in range(8):
+        onehot = (label_col == SG[blk, 0:1, :]).astype(F32).T
+        before = dot(earlier, onehot.astype(BF16)) + running
+        running = running + jnp.sum(onehot, axis=0, keepdims=True)
+        rank = jnp.sum(before * onehot, axis=1, keepdims=True)
+        limit = jnp.sum(onehot * lens, axis=1, keepdims=True)
+        ident = jnp.sum(label_row * onehot, axis=1, keepdims=True)
+        CODE[blk] = jnp.broadcast_to(jnp.where(rank < limit, ident, -1.0), (ROWS, LANES))
+
+    @pl.when(jnp.logical_not(native))
+    def _():
+        arrive(GM.at[j], sem_pc)
+
+    is_real = CODE[j][:, 0:1] >= 0.0
+    GM[j] = jnp.where(is_real, GM[j].astype(F32), 0.0).astype(BF16)
+    gather_g = Gather(GM)
+
+    spread_q.finish()
+    for i in range(32):
+        for ch in range(3):
+            WQ[i * 32 : (i + 1) * 32, ch * LANES : (ch + 1) * LANES] = RQ[
+                (i // 16) * 2 + (i // 4) % 2, ((i // 8) % 2) * 4 + i % 4, ch]
+    gather_g.start()
+    bias_q, bias_v = FULL[j][2:3, :], FULL[j][3:4, :]
+
+    def project(k, carry):
+        rows = pl.ds(pl.multiple_of(k * 256, 256), 256)
+        normed = N1[pl.ds(k * 2, 2)].reshape(256, D)
+        mixed = dot(normed, WQ[...])
+        queries = (mixed[:, :LANES] + bias_q).astype(BF16).astype(F32) * (HEAD_DIM ** -0.5)
+        keys = mixed[:, LANES : 2 * LANES]
+        values = mixed[:, 2 * LANES :] + bias_v
+        QS[rows] = queries.astype(BF16)
+        KK[rows] = keys.astype(BF16)
+        VV[rows] = values.astype(BF16)
+        QT[:, rows] = queries.T.astype(BF16)
+        KT[:, rows] = keys.T.astype(BF16)
+        VT[:, rows] = values.T.astype(BF16)
+        return carry
+
+    lax.fori_loop(0, 4, project, 0)
+
+    for slot in range(4):
+        @pl.when(jnp.logical_and(is_root, jnp.logical_not(jnp.logical_and(zl == c, l == slot))))
+        def _():
+            arrive(WO.at[slot], sem_wo + slot)
+
+    @pl.when(is_root)
+    def _():
+        for dx, dzh in ((0, 1), (1, 0), (1, 1)):
+            send(WO, WO, dev(dx=dx, dzh=dzh), sem_wt + dx * 2 + dzh)
+
+    for dc, dl in group_masks:
+        arrive(RI.at[t, flip(c, dc) * 4 + flip_l(dl)], sem_wi + dc * 4 + dl)
+    spread_i, spread_d = Spread(RI), Spread(WD)
+    spread_i.start()
+    spread_d.start()
+
+    @pl.when(jnp.logical_not(is_root))
+    def _():
+        arrive(WO, sem_wt + root_mask)
+
+    def pair_lanes(lp):
+        return (pl.ds(pl.multiple_of(lp * LANES, LANES), LANES), pl.ds(pl.multiple_of(512 + lp * LANES, LANES), LANES))
+
+    def cat_lanes(ref, lp):
+        first, second = pair_lanes(lp)
+        return jnp.concatenate([ref[:, first], ref[:, second]], axis=1)
+
+    def cat_rows(ref, lp):
+        return jnp.concatenate([ref[lp], ref[4 + lp]], axis=0)
+
+    class Scatter:
+        def __init__(self, part, chip, number, before=None):
+            self.part, self.chip, self.number, self.before = part, chip, number, before
+            self.near, self.far = slots(4), slots(4)
+
+        def emit(self, m, value):
+            if self.before is not None:
+                left(self.part.at[m, 1 - c], self.before.near + m)
+            low = value.astype(BF16)
+            self.part[m, 0] = low[:ROWS]
+            self.part[m, 1] = low[ROWS:]
+            send(self.part.at[m, 1 - c], SB.at[self.number, m], dev(dc=1), self.near + m)
+
+        def reduce(self, m):
+            arrive(SB.at[self.number, m], self.near + m)
+            if m == 0:
+                return
+            if self.before is not None:
+                left(self.chip.at[m], self.before.far + m)
+            self.chip[m] = (self.part[m, c].astype(F32) + SB[self.number, m].astype(F32)).astype(BF16)
+            send(self.chip.at[m], RV.at[self.number, m], dev(dl=m), self.far + m)
+
+        def finish(self):
+            for m in (1, 2, 3):
+                arrive(RV.at[self.number, m], self.far + m)
+
+        def rows(self, rows):
+            total = self.part[0, c, rows].astype(F32) + SB[self.number, 0, rows].astype(F32)
+            for m in (1, 2, 3):
+                total += RV[self.number, m, rows].astype(F32)
+            return total
+
+        def close(self):
+            for m in range(4):
+                left(self.part.at[m, 1 - c], self.near + m)
+                if m:
+                    left(self.chip.at[m], self.far + m)
+
+    head_rows = lax.broadcasted_iota(jnp.int32, (LANES, 256), 0)
+    head_lanes = lax.broadcasted_iota(jnp.int32, (256, LANES), 1)
+
+    def only_rows(value, h):
+        return jnp.where((head_rows >= h * 64) & (head_rows < (h + 1) * 64), value, jnp.zeros_like(value))
+
+    def only_lanes(value, h):
+        return jnp.where((head_lanes >= h * 64) & (head_lanes < (h + 1) * 64), value, jnp.zeros_like(value))
+
+    scatter_a = Scatter(PA, CS, 0)
+    attend_order = (3, 1, 2, 0)
+    for k, m in enumerate(attend_order):
+        lp = flip_l(m)
+        queries_t = cat_lanes(QT, lp)
+        seg_q = jnp.concatenate([SG[lp, 0:1, :], SG[4 + lp, 0:1, :]], axis=1)
+        for h in range(2):
+            masked_t = only_rows(queries_t.astype(F32), h).astype(BF16)
+
+            def score(i, top):
+                rows = pl.ds(pl.multiple_of(i * ROWS, ROWS), ROWS)
+                value = dot(KK[rows], masked_t)
+                code = CODE[i]
+                allowed = jnp.concatenate([code, code], axis=1) == seg_q
+                value = jnp.where(allowed, value, NEGATIVE)
+                SC[rows] = value
+                return jnp.maximum(top, jnp.max(value.reshape(16, 8, 256), axis=0))
+
+            top = lax.fori_loop(0, 8, score, jnp.full((8, 256), NEGATIVE, F32))
+            top = jnp.max(top, axis=0, keepdims=True)
+
+            def expo(i, total):
+                rows = pl.ds(pl.multiple_of(i * ROWS, ROWS), ROWS)
+                value = jnp.exp(SC[rows] - top)
+                PT[m, h, rows] = value.astype(BF16)
+                return total + jnp.sum(value.reshape(16, 8, 256), axis=0)
+
+            total = lax.fori_loop(0, 8, expo, jnp.zeros((8, 256), F32))
+            inverse = 1.0 / jnp.sum(total, axis=0, keepdims=True)
+            INV[m, h] = jnp.broadcast_to(inverse, (8, 256))
+            OT[m, h * 64 : (h + 1) * 64] = dot(VT[h * 64 : (h + 1) * 64, :], PT[m, h]) * inverse
+        joined = OT[m]
+        OL[m] = joined.astype(BF16)
+        partial = dot(joined.T.astype(BF16), WO[...].reshape(LANES, D))
+        scatter_a.emit(m, partial)
+        if k:
+            scatter_a.reduce(attend_order[k - 1])
+        if k == 0:
+            for dl in (1, 2):
+                gather_g.forward(dl)
+        if k == 1:
+            gather_g.forward(3)
+        if k == 2:
+            spread_i.forward()
+        if k == 3:
+            spread_d.forward()
+    scatter_a.reduce(0)
+    scatter_a.finish()
+
+    gain2, shift2, bias_o = PV[5:6, :], PV[6:7, :], PV[4:5, :]
+    for r in range(4):
+        rows = pl.ds(r * 32, 32)
+        residual = X[j, rows].astype(F32) + scatter_a.rows(rows) + bias_o
+        XO[rows] = residual
+        normal, root, value = norm_rows(residual, gain2, shift2)
+        N2F[rows] = normal
+        RS_[rows] = jnp.broadcast_to(root, (32, LANES))
+        N2[j, rows] = value.astype(BF16)
+    gather_n = Gather(N2)
+    gather_n.start()
+
+    spread_i.finish()
+    spread_d.finish()
+    for i in range(32):
+        for ch in range(4):
+            WI[i * 32 : (i + 1) * 32, ch * LANES : (ch + 1) * LANES] = RI[
+                (i // 16) * 2 + (i // 4) % 2, ((i // 8) % 2) * 4 + i % 4, ch]
+    for dl in range(4):
+        gather_g.sibling(dl)
+    pick = lax.broadcasted_iota(jnp.int32, (16, LANES), 0) == 8 + l
+    bias_in = jnp.concatenate(
+        [
+            jnp.sum(jnp.where(pick, FULL[(ch // 2) * 4 + c * 2 + ch % 2], 0.0), axis=0, keepdims=True)
+            for ch in range(4)
+        ],
+        axis=1,
+    )
+    scatter_m = Scatter(PA, CS, 1, scatter_a)
+    scatter_b = Scatter(PB, CSB, 2)
+    BG[0:1] = jnp.zeros((1, 512), F32)
+
+    def mlp(m):
+        lp = flip_l(m)
+        first, second = pair_lanes(lp)
+        hidden = dot(cat_rows(N2, lp), WI[...]) + bias_in
+        phi_cap = 0.5 * (1.0 + lax.erf(hidden * 0.7071067811865476))
+        phi = jnp.exp(-0.5 * hidden * hidden) * 0.3989422804014327
+        act = hidden * phi_cap
+        slope = phi_cap + hidden * phi
+        HA[m] = act.astype(BF16)
+        act_t = act.T.astype(BF16)
+        HAT[:, first] = act_t[:, :ROWS]
+        HAT[:, second] = act_t[:, ROWS:]
+        grad_act = dot_nt(cat_rows(GM, lp), WD[...].reshape(512, D))
+        grad_pre = (grad_act * slope).astype(BF16)
+        GP[lp] = grad_pre[:ROWS]
+        GP[4 + lp] = grad_pre[ROWS:]
+        BG[0:1] += jnp.sum(grad_pre.astype(F32), axis=0, keepdims=True)
+        scatter_m.emit(m, dot_nt(grad_pre, WI[...]))
+
+    gather_n.sibling(0)
+    mlp(0)
+    gather_n.forward(1)
+    gather_n.forward(2)
+    scatter_m.reduce(0)
+    gather_n.sibling(1)
+    mlp(1)
+    gather_n.forward(3)
+    gather_n.sibling(2)
+    mlp(2)
+    scatter_m.reduce(1)
+    gather_n.sibling(3)
+    mlp(3)
+    scatter_m.reduce(2)
+    scatter_m.reduce(3)
+    for k, m in enumerate((1, 2, 3, 0)):
+        scatter_b.emit(m, dot(HA[m], WD[...].reshape(512, D)))
+        if k:
+            scatter_b.reduce((1, 2, 3, 0)[k - 1])
+    scatter_b.reduce(0)
+    scatter_m.finish()
+
+    def norm_back(grad, normal, root, gain):
+        scaled = grad * gain
+        return root * (scaled - jnp.mean(scaled, axis=-1, keepdims=True)
+                       - normal * jnp.mean(scaled * normal, axis=-1, keepdims=True))
+
+    sums = [jnp.zeros((1, D), F32) for _ in range(4)]
+    for r in range(4):
+        rows = pl.ds(r * 32, 32)
+        grad = scatter_m.rows(rows)
+        normal = N2F[rows]
+        top_grad = GM[j, rows].astype(F32)
+        grad_residual = top_grad + norm_back(grad, normal, RS_[rows][:, 0:1], gain2)
+        low = grad_residual.astype(BF16)
+        GB[j, rows] = low
+        N2F[rows] = grad_residual
+        for i, value in enumerate((grad * normal, grad, low.astype(F32), top_grad)):
+            sums[i] += jnp.sum(value, axis=0, keepdims=True)
+    vectors = {5: sums[0], 6: sums[1], 4: sums[2], 7: sums[3]}
+    gather_b = Gather(GB)
+    gather_b.start()
+
+    class Total:
+        def __init__(self, part, from_x, middle, from_z):
+            self.part, self.from_x, self.middle, self.from_z = part, from_x, middle, from_z
+            self.sem = slots(2)
+
+        def start(self):
+            half = pl.ds((1 - x) * 2, 2)
+            push(self.part.at[half], self.from_x, dev(dx=1), self.sem)
+
+        def second(self):
+            arrive(self.from_x, self.sem)
+            self.middle[...] = (
+                self.part[x * 2 + 1 - zh].astype(F32) + self.from_x[1 - zh].astype(F32)
+            ).astype(BF16)
+            push(self.middle, self.from_z, dev(dzh=1), self.sem + 1)
+
+        def result(self):
+            arrive(self.from_z, self.sem + 1)
+            return self.part[t].astype(F32) + self.from_x[zh].astype(F32) + self.from_z[...].astype(F32)
+
+    total_d = Total(GD, XD, HD, ZD)
+    total_i = Total(GI, XI, HI, ZI)
+    total_q = Total(GQ, XQ, HQ, ZQ)
+    for ch in range(4):
+        GD[ch] = dot(HAT[ch * LANES : (ch + 1) * LANES, :], GM[...].reshape(8 * ROWS, D)).astype(BF16)
+    total_d.start()
+    gather_b.forward(1)
+    gather_b.forward(2)
+    all_pre = GP[...].reshape(8 * ROWS, 512)
+    for blk in range(8):
+        product = dot_tn(N2[:, :, blk * LANES : (blk + 1) * LANES].reshape(8 * ROWS, LANES), all_pre).astype(BF16)
+        for r in range(4):
+            i = blk * 4 + r
+            for ch in range(4):
+                GI[(i // 16) * 2 + (i // 4) % 2, ((i // 8) % 2) * 4 + i % 4, ch] = product[
+                    r * 32 : (r + 1) * 32, ch * LANES : (ch + 1) * LANES]
+    total_i.start()
+    gather_b.forward(3)
+
+    bias_d = PV[7:8, :]
+    sem_out, sem_in = slots(), slots()
+    scatter_b.finish()
+    for r in range(4):
+        rows = pl.ds(r * 32, 32)
+        CSB[0, rows] = (XO[rows] + scatter_b.rows(rows) + bias_d).astype(BF16)
+
+    @pl.when(native)
+    def _():
+        out_block[...] = CSB[0]
+
+    @pl.when(jnp.logical_not(native))
+    def _():
+        send(CSB.at[0], out_block, partner, sem_out)
+
+    DK[...] = jnp.zeros_like(DK)
+    DV[...] = jnp.zeros_like(DV)
+    GOF[...] = jnp.zeros_like(GOF)
+    for k, m in enumerate((0, 1, 2, 3)):
+        gather_b.sibling(m)
+        lp = flip_l(m)
+        first, second = pair_lanes(lp)
+        branch = cat_rows(GB, lp)
+        grad_att = dot_nt(branch, WO[...].reshape(LANES, D)).astype(BF16).astype(F32)
+        GOF[...] += dot(OL[m], branch)
+        grad_att_t = grad_att.T
+        both = grad_att_t * OT[m]
+        queries = jnp.concatenate([QS[first], QS[second]], axis=0).astype(F32)
+        for h in range(2):
+            inverse = INV[m, h][0:1]
+            delta = jnp.sum(both[h * 64 : (h + 1) * 64], axis=0, keepdims=True) * inverse
+            scaled_t = only_rows(grad_att_t * inverse, h)
+            scaled_low_t = scaled_t.astype(BF16)
+            scaled_low = scaled_t.T.astype(BF16)
+            queries_h = only_lanes(queries, h).astype(BF16)
+
+            def back(i, carry):
+                rows = pl.ds(i * ROWS, ROWS)
+                probs = PT[m, h, rows]
+                value = dot(VV[rows], scaled_low_t)
+                grad_scores = (probs.astype(F32) * (value - delta)).astype(BF16)
+                DV[rows] += dot(probs, scaled_low)
+                DK[rows] += dot(grad_scores, queries_h)
+                PT[m, h, rows] = grad_scores
+                return carry
+
+            for i in range(8):
+                back(i, 0)
+            DQ[h * 64 : (h + 1) * 64, :] = dot(KT[h * 64 : (h + 1) * 64, :], PT[m, h]) * (HEAD_DIM ** -0.5)
+        dq_rows = DQ[...].T.astype(BF16)
+        GMX[lp, :, 0:LANES] = dq_rows[:ROWS]
+        GMX[4 + lp, :, 0:LANES] = dq_rows[ROWS:]
+        if k == 0:
+            total_d.second()
+        if k == 2:
+            total_i.second()
+
+    GO[...] = GOF[...].astype(BF16)
+    sem_go, sem_gs = slots(4), slots(4)
+
+    @pl.when(jnp.logical_not(is_root))
+    def _():
+        send(GO, XGO.at[root_mask], (c * 2 + c, y * 4 + l), sem_go + root_mask)
+
+    for blk in range(8):
+        rows = pl.ds(blk * ROWS, ROWS)
+        GMX[blk, :, LANES : 2 * LANES] = DK[rows].astype(BF16)
+        GMX[blk, :, 2 * LANES :] = DV[rows].astype(BF16)
+
+    scatter_n = Scatter(PA, CS, 3, scatter_m)
+    for k, m in enumerate(attend_order):
+        scatter_n.emit(m, dot_nt(cat_rows(GMX, flip_l(m)), WQ[...]))
+        if k:
+            scatter_n.reduce(attend_order[k - 1])
+    all_mixed = GMX[...].reshape(8 * ROWS, 3 * LANES)
+    for blk in range(8):
+        product = dot_tn(N1[:, :, blk * LANES : (blk + 1) * LANES].reshape(8 * ROWS, LANES), all_mixed).astype(BF16)
+        for r in range(4):
+            i = blk * 4 + r
+            for ch in range(3):
+                GQ[(i // 16) * 2 + (i // 4) % 2, ((i // 8) % 2) * 4 + i % 4, ch] = product[
+                    r * 32 : (r + 1) * 32, ch * LANES : (ch + 1) * LANES]
+        if blk == 1:
+            scatter_n.reduce(0)
+    total_q.start()
+
+    out_d[...] = total_d.result()
+    TI[...] = total_i.result().astype(BF16)
+    sem_ti, sem_tq = slots(8), slots(8)
+    for dc, dl in group_masks:
+        peer_j = flip(c, dc) * 4 + flip_l(dl)
+        push(TI.at[peer_j], RGI.at[j], dev(dc=dc, dl=dl), sem_ti + dc * 4 + dl)
+    RGI[j] = TI[j]
+
+    @pl.when(is_root)
+    def _():
+        total = GOF[...]
+        for mask in (1, 2, 3):
+            arrive(XGO.at[mask], sem_go + mask)
+            total += XGO[mask].astype(F32)
+        TGO[...] = total.astype(BF16).reshape(4, 32, D)
+        for slot in range(4):
+            mine = jnp.logical_and(zl == c, l == slot)
+
+            @pl.when(mine)
+            def _():
+                RGO[...] = TGO[slot]
+
+            @pl.when(jnp.logical_not(mine))
+            def _():
+                send(TGO.at[slot], RGO, (x * 2 + zl, zh * 4 + slot), sem_gs + slot)
+
+    scatter_n.finish()
+    sums = [jnp.zeros((1, D), F32) for _ in range(2)]
+    for r in range(4):
+        rows = pl.ds(r * 32, 32)
+        grad = scatter_n.rows(rows)
+        normal, root, _ = norm_rows(X[j, rows].astype(F32), gain1, shift1)
+        XO[rows] = N2F[rows] + norm_back(grad, normal, root, gain1)
+        for i, value in enumerate((grad * normal, grad)):
+            sums[i] += jnp.sum(value, axis=0, keepdims=True)
+    vectors[0], vectors[1] = sums
+    left(CSB.at[1], scatter_b.far + 1)
+    CSB[1] = XO[...].astype(BF16)
+
+    @pl.when(native)
+    def _():
+        out_input[...] = CSB[1]
+
+    @pl.when(jnp.logical_not(native))
+    def _():
+        send(CSB.at[1], out_input, partner, sem_in)
+
+    mixed_sums = jnp.sum(all_mixed.astype(F32), axis=0, keepdims=True)
+    for q in range(8):
+        VG[q] = jnp.zeros((16, LANES), F32)
+        for p in (0, 1, 4, 5, 6, 7):
+            VG[q, p : p + 1] = vectors[p][:, q * LANES : (q + 1) * LANES]
+        for p, ch in ((2, 0), (3, 2)):
+            VG[q, p : p + 1] = jnp.where(j == q, mixed_sums[:, ch * LANES : (ch + 1) * LANES], 0.0)
+        ch = (q // 4) * 2 + q % 2
+        for r in range(4):
+            here = jnp.logical_and(c == (q // 2) % 2, l == r)
+            VG[q, 8 + r : 9 + r] = jnp.where(here, BG[0:1, ch * LANES : (ch + 1) * LANES], 0.0)
+    sem_v1, sem_v2 = slots(8), slots(4)
+    for dx, dc, dzh in line_masks:
+        mask = dx * 4 + dc * 2 + dzh
+        push(VG.at[flip(x, dx) * 4 + flip(c, dc) * 2 + flip(zh, dzh)], VR.at[mask], dev(dx=dx, dc=dc, dzh=dzh), sem_v1 + mask)
+
+    total_q.second()
+    for dc, dl in group_masks:
+        arrive(RGI.at[flip(c, dc) * 4 + flip_l(dl)], sem_ti + dc * 4 + dl)
+    for jj in range(8):
+        for ch in range(4):
+            flat = (ch // 2) * 16 + (jj // 4) * 8 + (ch % 2) * 4 + jj % 4
+            out_i[:, flat * LANES : (flat + 1) * LANES] = RGI[jj, ch].astype(F32)
+
+    slab = VG[q_own]
+    for dx, dc, dzh in line_masks:
+        mask = dx * 4 + dc * 2 + dzh
+        arrive(VR.at[mask], sem_v1 + mask)
+        slab += VR[mask]
+    SL[...] = slab
+    for dl in (1, 2, 3):
+        push(SL, SLR.at[dl], dev(dl=dl), sem_v2 + dl)
+
+    from_self = jnp.logical_and(x == c, l == pair_l)
+
+    @pl.when(jnp.logical_not(from_self))
+    def _():
+        arrive(RGO, sem_gs + l)
+
+    out_o[...] = RGO[...].astype(F32)
+
+    TQ[...] = total_q.result().astype(BF16)
+    for dc, dl in group_masks:
+        peer_j = flip(c, dc) * 4 + flip_l(dl)
+        push(TQ.at[peer_j], RGQ.at[j], dev(dc=dc, dl=dl), sem_tq + dc * 4 + dl)
+    RGQ[j] = TQ[j]
+
+    for dl in (1, 2, 3):
+        arrive(SLR.at[dl], sem_v2 + dl)
+        slab += SLR[dl]
+    out_small[...] = slab
+
+    for dc, dl in group_masks:
+        arrive(RGQ.at[flip(c, dc) * 4 + flip_l(dl)], sem_tq + dc * 4 + dl)
+    for jj in range(8):
+        for ch in range(3):
+            out_q[:, ch * D + jj * LANES : ch * D + (jj + 1) * LANES] = RGQ[jj, ch].astype(F32)
+
+    @pl.when(jnp.logical_not(native))
+    def _():
+        left(sgin, sem_ps)
+        left(xin, sem_px)
+        left(cin, sem_pc)
+        left(CSB.at[0], sem_out)
+        left(CSB.at[1], sem_in)
+        arrive(out_block, sem_out)
+        arrive(out_input, sem_in)
+
+    @pl.when(jnp.logical_not(to_self))
+    def _():
+        left(wo, sem_wo + l)
+
+    @pl.when(jnp.logical_not(is_root))
+    def _():
+        left(GO, sem_go + root_mask)
+
+    @pl.when(is_root)
+    def _():
+        for mask in (1, 2, 3):
+            left(WO, sem_wt + mask)
+        for slot in range(4):
+            @pl.when(jnp.logical_not(jnp.logical_and(zl == c, l == slot)))
+            def _():
+                left(TGO.at[slot], sem_gs + slot)
+
+    scatter_n.close()
+    for m in range(4):
+        left(PB.at[m, 1 - c], scatter_b.near + m)
+        if m > 1:
+            left(CSB.at[m], scatter_b.far + m)
+    for copy in pending:
+        copy.wait_send()
+
+
+def fused_scratch(copies):
+    def v(*shape, dtype=BF16):
+        return pltpu.VMEM(shape, dtype)
+
+    def f(*shape):
+        return pltpu.VMEM(shape, F32)
+
+    blocks = (8, ROWS, D)
+    return [
+        v(*blocks), v(*blocks), v(*blocks), v(*blocks), v(*blocks),
+        f(8, 8, LANES), f(4, 16, LANES), f(8, 16, LANES), f(16, D),
+        v(8, 3, 32, LANES), v(4, 8, 3, 32, LANES), v(D, 3 * LANES), v(4, 32, D),
+        v(8, 4, 32, LANES), v(4, 8, 4, 32, LANES), v(D, 512), v(4, LANES, D),
+        v(D, LANES), v(D, LANES), v(D, LANES), v(LANES, D), v(LANES, D), v(LANES, D),
+        f(8, ROWS, LANES), f(D, 256), v(4, 2, D, 256), f(4, 2, 8, 256),
+        f(4, LANES, 256), v(4, LANES, 256),
+        v(4, 2, ROWS, D), v(4, ROWS, D), v(4, 2, ROWS, D), v(4, ROWS, D),
+        v(4, 4, ROWS, D), v(4, 4, ROWS, D), f(ROWS, D), f(ROWS, D),
+        v(512, D), v(4, 256, 512), v(8, ROWS, 512),
+        f(D, LANES), f(D, LANES), f(LANES, 256), v(8, ROWS, 3 * LANES),
+        v(4, 8, 3, 32, LANES), v(4, 8, 4, 32, LANES), v(4, LANES, D),
+        v(2, 8, 3, 32, LANES), v(2, 8, 4, 32, LANES), v(2, LANES, D),
+        v(8, 3, 32, LANES), v(8, 4, 32, LANES), v(LANES, D),
+        v(8, 3, 32, LANES), v(8, 4, 32, LANES), v(LANES, D),
+        v(8, 3, 32, LANES), v(8, 4, 32, LANES),
+        v(8, 3, 32, LANES), v(8, 4, 32, LANES),
+        v(LANES, D), f(LANES, D), v(4, LANES, D), v(4, 32, D), v(32, D),
+        f(8, 16, LANES), f(8, 16, LANES), f(16, LANES), f(4, 16, LANES), f(ROWS, LANES), f(8, 512),
+        pltpu.SemaphoreType.DMA((copies,)),
+        pltpu.SemaphoreType.DMA((copies,)),
+    ]
+
+
+def fused_shards(
+    block_in,
+    attention_norm_gain,
+    attention_norm_bias,
+    query_key_value,
+    query_bias,
+    value_bias,
+    output_weight,
+    output_bias,
+    mlp_norm_gain,
+    mlp_norm_bias,
+    mlp_in_weight,
+    mlp_in_bias,
+    mlp_out_weight,
+    mlp_out_bias,
+    cotangent,
+    segment_ids,
+    sub_lengths,
+):
+    place = lax.rem(lax.axis_index("band"), 4)
+    small = jnp.stack(
+        [
+            attention_norm_gain, attention_norm_bias, query_bias, value_bias,
+            output_bias, mlp_norm_gain, mlp_norm_bias, mlp_out_bias,
+        ]
+    ).astype(F32)
+    spread = (jnp.arange(LANES) // 32 == place)[None, :]
+    packed = jnp.concatenate(
+        [
+            jnp.where(spread, jnp.tile(small, (1, 4)), 0.0),
+            jnp.where((jnp.arange(8) == place)[:, None], mlp_in_bias.astype(F32)[None, :], 0.0),
+        ]
+    )
+    slots = jnp.concatenate(
+        [
+            segment_ids.astype(F32),
+            jnp.pad(sub_lengths.astype(F32), ((0, 6), (0, LANES - SUBGRIDS))),
+        ]
+    )
+    copies = 200
+    vmem = pl.BlockSpec(memory_space=pltpu.VMEM)
+    block, grad_in, grad_q, grad_o, grad_i, grad_d, grad_small = pl.pallas_call(
+        functools.partial(fused_kernel, copies),
+        out_shape=(
+            jax.ShapeDtypeStruct((ROWS, D), BF16),
+            jax.ShapeDtypeStruct((ROWS, D), BF16),
+            jax.ShapeDtypeStruct((32, 3 * D), F32),
+            jax.ShapeDtypeStruct((32, D), F32),
+            jax.ShapeDtypeStruct((32, 4 * D), F32),
+            jax.ShapeDtypeStruct((LANES, D), F32),
+            jax.ShapeDtypeStruct((16, LANES), F32),
+        ),
+        in_specs=[vmem] * 8,
+        out_specs=(vmem,) * 7,
+        scratch_shapes=fused_scratch(copies),
+        compiler_params=pltpu.CompilerParams(
+            collective_id=0, has_side_effects=True, vmem_limit_bytes=63 * 2**20
+        ),
+    )(
+        block_in[0], cotangent[0], slots, packed,
+        query_key_value, output_weight, mlp_in_weight, mlp_out_weight,
+    )
+    mine = lax.dynamic_slice(grad_small, (0, place * 32), (8, 32))
+    grad_up_bias = lax.dynamic_index_in_dim(grad_small, 8 + place, 0, False)
+    return (
+        block[None], grad_in[None], mine[0], mine[1], grad_q, mine[2], mine[3], grad_o,
+        mine[4], mine[5], mine[6], grad_i, grad_up_bias, grad_d, mine[7],
+    )
+
+
 def solution(mesh):
+    small_slice = dict(mesh.shape) == {"seq": 4, "band": 8}
     return jax.shard_map(
-        shards,
+        fused_shards if small_slice else shards,
         mesh=mesh,
         in_specs=(
             P("seq", "band", None),

time: 1540 us -> 228 us (0.15)
  waiting for transfers between devices: 1110 us -> 0 us
  blocking collectives: 250 us -> 0 us
  Pallas kernels: 0 us -> 213 us
  matrix products: 109 us -> 0 us
  local copies, waits for them, and re-layouts: 36.9 us -> 11.4 us
    reduce_scatter x4 -> x0, waiting for transfers between devices: 884 us -> none  [the longest x1 361 us: shards(): lax.psum_scatter(grad_up_weight, ('seq', 'band'), scatter_dimension=0, ti...]
    all_gather x8 -> x0, waiting for transfers between devices: 224 us -> none  [the longest x1 76.7 us: shards(): lax.all_gather(mlp_in_weight, ('seq', 'band'), axis=0, tiled=True)]
    pallas_call x0 -> x1, Pallas kernels: none -> 213 us  [fused_shards(): pl.pallas_call(functools.partial(fused_kernel, copies), out_shape=(jax.Sh...]
    all_gather x5 -> x0, blocking collectives: 148 us -> none  [the longest x1 60.9 us: shards(): lax.all_gather(mlp_in_bias, ('seq', 'band'), axis=0, tiled=True)]
    dot_general x18 -> x0, matrix products: 109 us -> none  [the longest x1 10.1 us: key_step(): jnp.einsum('hqk,khe->qhe', grad_scores, key_part, preferred_element_type=...]
    unnamed x3 -> x0, blocking collectives: 102 us -> none
  transfers between devices with their start and end apart: 12 -> 0, of which waited for: 8 -> 0; matrix products, arithmetic and copies ran while one was open for 10% -> 0% of each run, Pallas kernels for 0% -> 0%
where the time goes in v1:
time: 228 us; the launch traced here: 227 us
  Pallas kernels  213 us (93%)
  local copies, waits for them, and re-layouts  11.4 us (5%)
    pallas_call x1, Pallas kernels, fused_shards(): pl.pallas_call(functools.partial(fused_kernel, copies), out_shape=(jax.Sh...  213 us
    unnamed x40, local copies, waits for them, and re-layouts  9.46 us

profile of v1, /device:TPU:1, one launch (start us, length us, event | category | flops | bytes accessed | tf_op | source)
XLA Modules:
  0.0 226.6 jit_solution(15981367122549511200)
XLA Ops:
  0.7 0.6 copy-done.14
  1.3 0.7 copy-done.15
  2.0 0.7 copy-done.16
  2.6 0.0 copy-start.11
  2.6 0.0 copy-start.12
  2.7 0.0 copy-start.6
  2.7 0.0 copy-start.7
  2.7 0.6 copy-done.13
  3.3 0.0 copy-done.9
  3.3 0.0 copy-done.10
  3.3 0.0 copy-done.11
  3.3 0.0 copy-done.12
  3.3 0.0 copy-done.6
  3.4 0.0 copy-done.7
  3.4 0.0 copy-done.8
  3.4 0.6 select_maximum_fusion.refs_2_
  4.0 0.1 tile.10
  4.1 0.1 broadcast_select_fusion
  4.2 0.6 pad_maximum_fusion.refs_3_
  4.8 213.1 %shard_map.280 = (bf16[128,1024]{1,0:T(8,128)(2,1)}, bf16[128,1024]{1,0:T(8,128)(2,1)}, f32[32,3072]{1,0:T(8,128)}, f32[32,1024]{1,0:T(8,128)}, f32[32,4096]{1,0...) custom-call(bf16[128,1024]{1,0:T(8,128)(2,1)} %bitcast.30, bf16[128,1024]{1,0:T(8,128)(2,1)} %bitcast.31, ...), custom_call_target="tpu_custom_call" | custom-call | tf_op jit(solution)/shard_map/pallas_call | solution.py:1237
  217.9 1.2 dynamic-slice_bitcast_fusion
  219.1 0.7 copy-done.5
  219.8 0.1 constant_dynamic-slice_fusion
  219.9 0.5 slice_bitcast_fusion
  220.5 1.7 copy.38
  222.2 0.7 copy.39
  222.9 0.7 copy.40
  223.7 0.2 copy-done.4
  223.9 0.7 copy.41
  224.6 0.8 copy.42
  225.4 0.4 copy-done
  225.8 0.8 copy.43
  (23 shorter events, 0.1 us)
Async XLA Ops:
  0.7 0.7 copy-start.14
  1.3 0.7 copy-start.15
  2.0 0.7 copy-start.16
  2.6 0.7 copy-start.13
  2.6 0.7 copy-start.9
  2.6 0.7 copy-start.10
  2.6 0.7 copy-start.11
  2.6 0.7 copy-start.12
  2.7 0.7 copy-start.6
  2.7 0.7 copy-start.7
  2.7 0.7 copy-start.8
  219.1 0.7 copy-start.5
  220.5 1.7 copy-start.3
  220.5 2.4 %copy-start.2 = (f32[32,3072]{1,0:T(8,128)S(1)}, f32[32,3072]{1,0:T(8,128)}, u32[]{:S(2)}) copy-start(f32[32,3072]{1,0:T(8,128)} %get-tuple-element.58) | copy-start | bytes 1179652
  222.9 1.0 copy-start.4
  222.9 1.7 copy-start.1
  224.6 1.2 copy-start

commit v2 on v1

--- a/solution.py
+++ b/solution.py
@@ -375,6 +375,7 @@
 MESH_ID = pl.DeviceIdType.MESH
 ROWS = 128
 LANES = 128
+COPIES = 240
 
 
 def dot(lhs, rhs):
@@ -389,19 +390,28 @@
     return lax.dot_general(lhs, rhs, (((0,), (0,)), ((), ())), preferred_element_type=F32)
 
 
+def flat_column(jj, ch):
+    return (ch // 2) * 16 + (jj // 4) * 8 + (ch % 2) * 4 + jj % 4
+
+
+def shard_place(i):
+    return (i // 16) * 2 + (i // 4) % 2, ((i // 8) % 2) * 4 + i % 4
+
+
 def fused_kernel(copies, *refs):
     (
-        xin, cin, sgin, pkin, wq, wo, wi, wd,
+        xin, cin, seg_in, len_in, wq, wo, wi, wd,
+        p0, p1, p2, p3, p4, p5, p6, p7, pb,
         out_block, out_input, out_q, out_o, out_i, out_d, out_small,
-        X, N1, N2, GM, GB, SG, SP, FULL, PV,
-        WSQ, RQ, WQ, WO, WSI, RI, WI, WD,
+        X, N0, N1, N2, GM, GB, SGI, SG, PK, SP, FULL, PV,
+        WQI, WSQ, RQ, WQ, WO, WII, WSI, RI, WI, WD,
         QS, KK, VV, QT, KT, VT, CODE, SC, PT, INV, OT, OL,
-        PA, CS, PB, CSB, SB, RV, XO, N2F, HAT, HA, GP,
+        PA, CS, PB, CSB, SB, RV, XO, N2F, HAT, HA, GP, GA,
         DK, DV, DQ, GMX,
-        GQ, GI, GD, XQ, XI, XD, HQ, HI, HD, ZQ, ZI, ZD, TQ, TI, RGQ, RGI,
-        GO, GOF, XGO, TGO, RGO,
-        VG, VR, SL, SLR, RS_, BG,
-        ssem, rsem,
+        GQ, GI, GD, XQ, XI, XD, HQ, HI, HD, ZQ, ZI, ZD, TQ, TI, TD,
+        GO, GOF, XGO, TGO,
+        VG, VR, SL, SLR, SLF, RS_, BG, BO, BI,
+        ssem, rsem, lsem,
     ) = refs
     s = lax.axis_index("seq")
     b = lax.axis_index("band")
@@ -419,6 +429,8 @@
     def dev(dx=0, dc=0, dzh=0, dl=0):
         return (flip(x, dx) * 2 + flip(c, dc), flip(zh, dzh) * 4 + flip_l(dl))
 
+    roles = (l, flip_l(2), flip_l(1), flip_l(3))
+
     counter = [0]
     pending = []
 
@@ -450,79 +462,123 @@
             src_ref=src, dst_ref=src, send_sem=ssem.at[sem], recv_sem=rsem.at[sem],
             device_id=dev(dc=1), device_id_type=MESH_ID).wait_send()
 
-    group_masks = [(dc, dl) for dl in (1, 2, 3, 0) for dc in (0, 1) if (dc, dl) != (0, 0)]
-    line_masks = [(dx, dc, dzh) for dx in (0, 1) for dc in (0, 1) for dzh in (0, 1) if dx + dc + dzh]
+    def move(src, dst, sem):
+        return pltpu.make_async_copy(src, dst, lsem.at[sem])
+
+    group_masks = [(dc, dl) for dl in (3, 1, 2, 0) for dc in (0, 1) if (dc, dl) != (0, 0)]
+    line_masks = [(dx, dc, dzh) for dx in (1, 0) for dc in (0, 1) for dzh in (1, 0) if dx + dc + dzh]
+
+    def group(dc, dl):
+        return flip(c, dc) * 4 + flip_l(dl)
+
+    native = c == zh
+    foreign = jnp.logical_not(native)
+    partner = dev(dc=1, dzh=1)
+    their_block = (1 - c) * 4 + l
 
     barrier = pltpu.get_barrier_semaphore()
     peers = [dict(dc=dc, dl=dl) for dc, dl in group_masks]
     peers += [dict(dx=a, dc=e, dzh=f) for a, e, f in line_masks if (a, e, f) != (0, 1, 0)]
     for peer in peers:
         pl.semaphore_signal(barrier, inc=1, device_id=dev(**peer), device_id_type=MESH_ID)
-    pl.semaphore_wait(barrier, len(peers))
-
-    native = c == zh
-    partner = dev(dc=1, dzh=1)
-    their_block = (1 - c) * 4 + l
-
-    sem_px, sem_pc, sem_ps = slots(), slots(), slots()
+    get_q, get_i, get_d = move(wq, WQI, 0), move(wi, WII, 1), move(wd, WD.at[t], 2)
+    get_x, get_c = move(xin.at[0], X.at[j], 3), move(cin.at[0], GM.at[j], 4)
+    get_q.start()
+    get_i.start()
+    get_d.start()
 
     @pl.when(native)
     def _():
-        X[j] = xin[...]
-        SG[j] = sgin[...]
-
-    @pl.when(jnp.logical_not(native))
-    def _():
-        send(sgin, SG.at[their_block], partner, sem_ps)
-        send(xin, X.at[their_block], partner, sem_px)
-
-    sem_s1 = slots(4)
-    for dl in (1, 2, 3):
-        push(pkin, SP.at[dl], dev(dl=dl), sem_s1 + dl)
-
+        get_x.start()
+        get_c.start()
+
+    lane_group = lax.broadcasted_iota(jnp.int32, (1, LANES), 1) // 32
+    PK[...] = jnp.zeros_like(PK)
+    for p, ref in enumerate((p0, p1, p2, p3, p4, p5, p6, p7)):
+        value = ref[...].astype(F32).reshape(1, 32)
+        PK[p : p + 1] = jnp.where(lane_group == l, jnp.concatenate([value] * 4, axis=1), 0.0)
+    own_bias = pb[...].astype(F32).reshape(1, LANES)
+    for r in range(4):
+        PK[8 + r : 9 + r] = jnp.where(l == r, own_bias, jnp.zeros_like(own_bias))
+    SGI[...] = jnp.zeros_like(SGI)
+    SGI[0:1] = seg_in[...].astype(F32)
+    SGI[1:2, 0:SUBGRIDS] = len_in[...].astype(F32)
+    get_q.wait()
     for jj in range(8):
         for ch in range(3):
-            WSQ[jj, ch] = wq[:, ch * D + jj * LANES : ch * D + (jj + 1) * LANES]
-    sem_wq = slots(8)
+            WSQ[jj, ch] = WQI[:, ch * D + jj * LANES : ch * D + (jj + 1) * LANES]
+    for ch in range(3):
+        RQ[ch, t, j] = WSQ[j, ch]
+    pl.semaphore_wait(barrier, len(peers))
+
+    sem_px, sem_pc, sem_ps = slots(), slots(), slots()
+    sem_wq, sem_s1 = slots(8), slots(4)
+    for dl in (1, 2, 3):
+        push(PK, SP.at[dl], dev(dl=dl), sem_s1 + dl)
+
+    @pl.when(native)
+    def _():
+        SG[j] = SGI[...]
+
+    @pl.when(foreign)
+    def _():
+        send(SGI, SG.at[their_block], partner, sem_ps)
+        send(xin.at[0], X.at[their_block], partner, sem_px)
+
     for dc, dl in group_masks:
-        peer_j = flip(c, dc) * 4 + flip_l(dl)
-        push(WSQ.at[peer_j], RQ.at[t, j], dev(dc=dc, dl=dl), sem_wq + dc * 4 + dl)
-    RQ[t, j] = WSQ[j]
+        push(WSQ.at[group(dc, dl)], RQ.at[:, t, j], dev(dc=dc, dl=dl), sem_wq + dc * 4 + dl)
 
     class Gather:
         def __init__(self, buf):
             self.buf, self.far, self.near = buf, slots(4), slots(4)
 
         def start(self):
-            for dl in (1, 2, 3):
-                push(self.buf.at[j], self.buf.at[j], dev(dl=dl), self.far + dl)
-            push(self.buf.at[j], self.buf.at[j], dev(dc=1), self.near)
-
-        def forward(self, dl):
-            block = self.buf.at[c * 4 + flip_l(dl)]
-            arrive(block, self.far + dl)
-            push(block, block, dev(dc=1), self.near + dl)
-
-        def sibling(self, dl):
-            arrive(self.buf.at[(1 - c) * 4 + flip_l(dl)], self.near + dl)
-
-    @pl.when(jnp.logical_not(native))
-    def _():
-        arrive(SG.at[j], sem_ps)
-
-    sem_sg = slots(8)
-    for dc, dl in group_masks:
-        push(SG.at[j], SG.at[j], dev(dc=dc, dl=dl), sem_sg + dc * 4 + dl)
-
-    @pl.when(jnp.logical_not(native))
-    def _():
-        arrive(X.at[j], sem_px)
+            block = self.buf.at[j]
+            copies_out = [
+                send(block, block, (s, zh * 4 + roles[1]), self.far + 1),
+                send(block, block, (s, zh * 4 + roles[2]), self.far + 2),
+                send(block, block, dev(dc=1), self.near),
+            ]
+            return copies_out
+
+        def begin(self):
+            pending.extend(self.start())
+
+        def forward(self, k):
+            block = self.buf.at[c * 4 + roles[k]]
+            arrive(block, self.far + k)
+            if k == 1:
+                push(block, block, (s, zh * 4 + roles[2]), self.far + 3)
+            push(block, block, dev(dc=1), self.near + k)
+
+        def sibling(self, k):
+            arrive(self.buf.at[(1 - c) * 4 + roles[k]], self.near + k)
 
     gather_x = Gather(X)
-    gather_x.start()
+    gather_g = Gather(GM)
+
+    @pl.when(native)
+    def _():
+        get_x.wait()
+        gather_x.start()
+
+    sem_wo, sem_wt = slots(4), slots(4)
+    pair_l = c * 2 + zh
+    to_self = jnp.logical_and(x == c, l == pair_l)
+    is_root = jnp.logical_and(x == c, zh == y)
+    root_mask = jnp.abs(x - c) * 2 + jnp.abs(zh - y)
+    get_o = move(wo, WO.at[l], 5)
+
+    @pl.when(to_self)
+    def _():
+        get_o.start()
+
+    @pl.when(jnp.logical_not(to_self))
+    def _():
+        send(wo, WO.at[l], (x * 2 + x, zh * 4 + pair_l), sem_wo + l)
 
     q_own = x * 4 + c * 2 + zh
-    slab = pkin[...]
+    slab = PK[...]
     for dl in (1, 2, 3):
         arrive(SP.at[dl], sem_s1 + dl)
         slab += SP[dl]
@@ -549,10 +605,39 @@
             arrive(self.buf.at[(1 - x) * 2 + zh], self.sem + 1)
             arrive(self.buf.at[(1 - x) * 2 + 1 - zh], self.sem + 2)
 
+    spread_q = [Spread(RQ.at[ch]) for ch in range(3)]
     for dc, dl in group_masks:
-        arrive(RQ.at[t, flip(c, dc) * 4 + flip_l(dl)], sem_wq + dc * 4 + dl)
-    spread_q = Spread(RQ)
-    spread_q.start()
+        arrive(RQ.at[:, t, group(dc, dl)], sem_wq + dc * 4 + dl)
+    for ch in range(3):
+        spread_q[ch].start()
+
+    sem_sg = slots(8)
+
+    @pl.when(foreign)
+    def _():
+        arrive(SG.at[j], sem_ps)
+
+    for dc, dl in group_masks:
+        push(SG.at[j], SG.at[j], dev(dc=dc, dl=dl), sem_sg + dc * 4 + dl)
+    @pl.when(foreign)
+    def _():
+        arrive(X.at[j], sem_px)
+        gather_x.start()
+
+    for slot in range(4):
+        @pl.when(jnp.logical_and(is_root, jnp.logical_not(jnp.logical_and(zl == c, l == slot))))
+        def _():
+            arrive(WO.at[slot], sem_wo + slot)
+
+    @pl.when(to_self)
+    def _():
+        get_o.wait()
+
+    @pl.when(is_root)
+    def _():
+        send(WO, WO, dev(dzh=1), sem_wt + 1)
+        send(WO, WO, dev(dx=1), sem_wt + 2)
+
 
     for dx, dc, dzh in line_masks:
         arrive(FULL.at[flip(x, dx) * 4 + flip(c, dc) * 2 + flip(zh, dzh)], sem_s2 + dx * 4 + dc * 2 + dzh)
@@ -568,63 +653,50 @@
         return normal, root, normal * gain + shift
 
     def norm_one(block):
-        def body(i, carry):
-            rows = pl.ds(pl.multiple_of(i * 32, 32), 32)
-            N1[block, rows] = norm_rows(X[block, rows].astype(F32), gain1, shift1)[2].astype(BF16)
-            return carry
-
-        lax.fori_loop(0, ROWS // 32, body, 0)
+        for r in range(2):
+            rows = pl.ds(r * 64, 64)
+            normal, _, value = norm_rows(X[block, rows].astype(F32), gain1, shift1)
+            N0[block, rows] = normal.astype(BF16)
+            N1[block, rows] = value.astype(BF16)
 
     norm_one(j)
-    for dl in (1, 2):
-        gather_x.forward(dl)
+
     gather_x.sibling(0)
     norm_one((1 - c) * 4 + l)
-    norm_one(c * 4 + flip_l(1))
+    gather_x.forward(1)
+    gather_x.forward(2)
+    norm_one(c * 4 + roles[1])
+    norm_one(c * 4 + roles[2])
+    spread_q[0].forward()
+    for k in (1, 2):
+        gather_x.sibling(k)
     gather_x.forward(3)
-    norm_one(c * 4 + flip_l(2))
-    spread_q.forward()
-
-    @pl.when(native)
-    def _():
-        GM[j] = cin[...]
-
-    @pl.when(jnp.logical_not(native))
-    def _():
-        send(cin, GM.at[their_block], partner, sem_pc)
-
-    sem_wi = slots(8)
+    norm_one((1 - c) * 4 + roles[1])
+    spread_q[1].forward()
+    norm_one((1 - c) * 4 + roles[2])
+    norm_one(c * 4 + roles[3])
+    spread_q[2].forward()
+    gather_x.sibling(3)
+    norm_one((1 - c) * 4 + roles[3])
+
+    @pl.when(foreign)
+    def _():
+        send(cin.at[0], GM.at[their_block], partner, sem_pc)
+
+    get_i.wait()
     for jj in range(8):
         for ch in range(4):
-            flat = (ch // 2) * 16 + (jj // 4) * 8 + (ch % 2) * 4 + jj % 4
-            WSI[jj, ch] = wi[:, flat * LANES : (flat + 1) * LANES]
+            flat = flat_column(jj, ch)
+            WSI[jj, ch] = WII[:, flat * LANES : (flat + 1) * LANES]
+    sem_wi = slots(8)
     for dc, dl in group_masks:
-        peer_j = flip(c, dc) * 4 + flip_l(dl)
-        push(WSI.at[peer_j], RI.at[t, j], dev(dc=dc, dl=dl), sem_wi + dc * 4 + dl)
+        push(WSI.at[group(dc, dl)], RI.at[t, j], dev(dc=dc, dl=dl), sem_wi + dc * 4 + dl)
     RI[t, j] = WSI[j]
-    WD[t] = wd[...]
-
-    sem_wo, sem_wt = slots(4), slots(4)
-    pair_l = c * 2 + zh
-    to_self = jnp.logical_and(x == c, l == pair_l)
-    is_root = jnp.logical_and(x == c, zh == y)
-    root_mask = jnp.abs(x - c) * 2 + jnp.abs(zh - y)
-
-    @pl.when(to_self)
-    def _():
-        WO[l] = wo[...]
-
-    @pl.when(jnp.logical_not(to_self))
-    def _():
-        send(wo, WO.at[l], (x * 2 + x, zh * 4 + pair_l), sem_wo + l)
-
-    for dl in (1, 2, 3):
-        gather_x.sibling(dl)
-        norm_one((1 - c) * 4 + flip_l(dl))
-    norm_one(c * 4 + flip_l(3))
+    get_d.wait()
+    spread_i, spread_d = Spread(RI), Spread(WD)
 
     for dc, dl in group_masks:
-        arrive(SG.at[flip(c, dc) * 4 + flip_l(dl)], sem_sg + dc * 4 + dl)
+        arrive(SG.at[group(dc, dl)], sem_sg + dc * 4 + dl)
     lens = SG[j, 1:2, :]
     row_ids = lax.broadcasted_iota(jnp.int32, (LANES, LANES), 0)
     lane_ids = lax.broadcasted_iota(jnp.int32, (LANES, LANES), 1)
@@ -641,25 +713,23 @@
         ident = jnp.sum(label_row * onehot, axis=1, keepdims=True)
         CODE[blk] = jnp.broadcast_to(jnp.where(rank < limit, ident, -1.0), (ROWS, LANES))
 
-    @pl.when(jnp.logical_not(native))
-    def _():
-        arrive(GM.at[j], sem_pc)
-
-    is_real = CODE[j][:, 0:1] >= 0.0
-    GM[j] = jnp.where(is_real, GM[j].astype(F32), 0.0).astype(BF16)
-    gather_g = Gather(GM)
-
-    spread_q.finish()
-    for i in range(32):
-        for ch in range(3):
-            WQ[i * 32 : (i + 1) * 32, ch * LANES : (ch + 1) * LANES] = RQ[
-                (i // 16) * 2 + (i // 4) % 2, ((i // 8) % 2) * 4 + i % 4, ch]
-    gather_g.start()
+    @pl.when(jnp.logical_not(is_root))
+    def _():
+        arrive(WO, sem_wt + root_mask)
+
+    @pl.when(root_mask == 1)
+    def _():
+        send(WO, WO, dev(dx=1), sem_wt + 3)
+
+    for ch in range(3):
+        spread_q[ch].finish()
+        for i in range(32):
+            tt, jj = shard_place(i)
+            WQ[i * 32 : (i + 1) * 32, ch * LANES : (ch + 1) * LANES] = RQ[ch, tt, jj]
     bias_q, bias_v = FULL[j][2:3, :], FULL[j][3:4, :]
-
-    def project(k, carry):
-        rows = pl.ds(pl.multiple_of(k * 256, 256), 256)
-        normed = N1[pl.ds(k * 2, 2)].reshape(256, D)
+    for k in range(4):
+        rows = pl.ds(k * 256, 256)
+        normed = N1[2 * k : 2 * k + 2].reshape(256, D)
         mixed = dot(normed, WQ[...])
         queries = (mixed[:, :LANES] + bias_q).astype(BF16).astype(F32) * (HEAD_DIM ** -0.5)
         keys = mixed[:, LANES : 2 * LANES]
@@ -670,29 +740,23 @@
         QT[:, rows] = queries.T.astype(BF16)
         KT[:, rows] = keys.T.astype(BF16)
         VT[:, rows] = values.T.astype(BF16)
-        return carry
-
-    lax.fori_loop(0, 4, project, 0)
-
-    for slot in range(4):
-        @pl.when(jnp.logical_and(is_root, jnp.logical_not(jnp.logical_and(zl == c, l == slot))))
-        def _():
-            arrive(WO.at[slot], sem_wo + slot)
-
-    @pl.when(is_root)
-    def _():
-        for dx, dzh in ((0, 1), (1, 0), (1, 1)):
-            send(WO, WO, dev(dx=dx, dzh=dzh), sem_wt + dx * 2 + dzh)
 
     for dc, dl in group_masks:
-        arrive(RI.at[t, flip(c, dc) * 4 + flip_l(dl)], sem_wi + dc * 4 + dl)
-    spread_i, spread_d = Spread(RI), Spread(WD)
+        arrive(RI.at[t, group(dc, dl)], sem_wi + dc * 4 + dl)
     spread_i.start()
     spread_d.start()
 
-    @pl.when(jnp.logical_not(is_root))
-    def _():
-        arrive(WO, sem_wt + root_mask)
+    @pl.when(native)
+    def _():
+        get_c.wait()
+
+    @pl.when(foreign)
+    def _():
+        arrive(GM.at[j], sem_pc)
+
+    is_real = CODE[j][:, 0:1] >= 0.0
+    GM[j] = jnp.where(is_real, GM[j].astype(F32), 0.0).astype(BF16)
+    gather_g.begin()
 
     def pair_lanes(lp):
         return (pl.ds(pl.multiple_of(lp * LANES, LANES), LANES), pl.ds(pl.multiple_of(512 + lp * LANES, LANES), LANES))
@@ -705,8 +769,8 @@
         return jnp.concatenate([ref[lp], ref[4 + lp]], axis=0)
 
     class Scatter:
-        def __init__(self, part, chip, number, before=None):
-            self.part, self.chip, self.number, self.before = part, chip, number, before
+        def __init__(self, part, chip, number, before=None, tree=True):
+            self.part, self.chip, self.number, self.before, self.tree = part, chip, number, before, tree
             self.near, self.far = slots(4), slots(4)
 
         def emit(self, m, value):
@@ -723,16 +787,21 @@
                 return
             if self.before is not None:
                 left(self.chip.at[m], self.before.far + m)
-            self.chip[m] = (self.part[m, c].astype(F32) + SB[self.number, m].astype(F32)).astype(BF16)
-            send(self.chip.at[m], RV.at[self.number, m], dev(dl=m), self.far + m)
+            total = self.part[m, c].astype(F32) + SB[self.number, m].astype(F32)
+            if self.tree and m == 2:
+                arrive(RV.at[self.number, 3], self.far + 3)
+                total += RV[self.number, 3].astype(F32)
+            self.chip[m] = total.astype(BF16)
+            device = dev(dl=1) if self.tree and m == 3 else dev(dl=m)
+            send(self.chip.at[m], RV.at[self.number, m], device, self.far + m)
 
         def finish(self):
-            for m in (1, 2, 3):
+            for m in (1, 2) if self.tree else (1, 2, 3):
                 arrive(RV.at[self.number, m], self.far + m)
 
         def rows(self, rows):
             total = self.part[0, c, rows].astype(F32) + SB[self.number, 0, rows].astype(F32)
-            for m in (1, 2, 3):
+            for m in (1, 2) if self.tree else (1, 2, 3):
                 total += RV[self.number, m, rows].astype(F32)
             return total
 
@@ -759,44 +828,31 @@
         seg_q = jnp.concatenate([SG[lp, 0:1, :], SG[4 + lp, 0:1, :]], axis=1)
         for h in range(2):
             masked_t = only_rows(queries_t.astype(F32), h).astype(BF16)
-
-            def score(i, top):
-                rows = pl.ds(pl.multiple_of(i * ROWS, ROWS), ROWS)
+            top = jnp.full((8, 256), NEGATIVE, F32)
+            for i in range(8):
+                rows = pl.ds(i * ROWS, ROWS)
                 value = dot(KK[rows], masked_t)
                 code = CODE[i]
                 allowed = jnp.concatenate([code, code], axis=1) == seg_q
                 value = jnp.where(allowed, value, NEGATIVE)
-                SC[rows] = value
-                return jnp.maximum(top, jnp.max(value.reshape(16, 8, 256), axis=0))
-
-            top = lax.fori_loop(0, 8, score, jnp.full((8, 256), NEGATIVE, F32))
+                SC[h, rows] = value
+                top = jnp.maximum(top, jnp.max(value.reshape(16, 8, 256), axis=0))
             top = jnp.max(top, axis=0, keepdims=True)
-
-            def expo(i, total):
-                rows = pl.ds(pl.multiple_of(i * ROWS, ROWS), ROWS)
-                value = jnp.exp(SC[rows] - top)
+            total = jnp.zeros((8, 256), F32)
+            for i in range(8):
+                rows = pl.ds(i * ROWS, ROWS)
+                value = jnp.exp(SC[h, rows] - top)
                 PT[m, h, rows] = value.astype(BF16)
-                return total + jnp.sum(value.reshape(16, 8, 256), axis=0)
-
-            total = lax.fori_loop(0, 8, expo, jnp.zeros((8, 256), F32))
+                total = total + jnp.sum(value.reshape(16, 8, 256), axis=0)
             inverse = 1.0 / jnp.sum(total, axis=0, keepdims=True)
             INV[m, h] = jnp.broadcast_to(inverse, (8, 256))
             OT[m, h * 64 : (h + 1) * 64] = dot(VT[h * 64 : (h + 1) * 64, :], PT[m, h]) * inverse
+            if k and h == 0:
+                scatter_a.reduce(attend_order[k - 1])
         joined = OT[m]
         OL[m] = joined.astype(BF16)
-        partial = dot(joined.T.astype(BF16), WO[...].reshape(LANES, D))
-        scatter_a.emit(m, partial)
-        if k:
-            scatter_a.reduce(attend_order[k - 1])
-        if k == 0:
-            for dl in (1, 2):
-                gather_g.forward(dl)
-        if k == 1:
-            gather_g.forward(3)
-        if k == 2:
-            spread_i.forward()
-        if k == 3:
-            spread_d.forward()
+        scatter_a.emit(m, dot(joined.T.astype(BF16), WO[...].reshape(LANES, D)))
+    spread_i.forward()
     scatter_a.reduce(0)
     scatter_a.finish()
 
@@ -810,16 +866,16 @@
         RS_[rows] = jnp.broadcast_to(root, (32, LANES))
         N2[j, rows] = value.astype(BF16)
     gather_n = Gather(N2)
-    gather_n.start()
-
+    gather_n.begin()
+
+    for k in (1, 2):
+        gather_g.forward(k)
+    spread_d.forward()
     spread_i.finish()
-    spread_d.finish()
     for i in range(32):
+        tt, jj = shard_place(i)
         for ch in range(4):
-            WI[i * 32 : (i + 1) * 32, ch * LANES : (ch + 1) * LANES] = RI[
-                (i // 16) * 2 + (i // 4) % 2, ((i // 8) % 2) * 4 + i % 4, ch]
-    for dl in range(4):
-        gather_g.sibling(dl)
+            WI[i * 32 : (i + 1) * 32, ch * LANES : (ch + 1) * LANES] = RI[tt, jj, ch]
     pick = lax.broadcasted_iota(jnp.int32, (16, LANES), 0) == 8 + l
     bias_in = jnp.concatenate(
         [
@@ -828,56 +884,99 @@
         ],
         axis=1,
     )
-    scatter_m = Scatter(PA, CS, 1, scatter_a)
+    scatter_m = Scatter(PA, CS, 1, scatter_a, tree=False)
     scatter_b = Scatter(PB, CSB, 2)
     BG[0:1] = jnp.zeros((1, 512), F32)
 
-    def mlp(m):
+    def hidden_part(m):
         lp = flip_l(m)
         first, second = pair_lanes(lp)
         hidden = dot(cat_rows(N2, lp), WI[...]) + bias_in
         phi_cap = 0.5 * (1.0 + lax.erf(hidden * 0.7071067811865476))
         phi = jnp.exp(-0.5 * hidden * hidden) * 0.3989422804014327
         act = hidden * phi_cap
-        slope = phi_cap + hidden * phi
+        GA[m] = phi_cap + hidden * phi
         HA[m] = act.astype(BF16)
         act_t = act.T.astype(BF16)
         HAT[:, first] = act_t[:, :ROWS]
         HAT[:, second] = act_t[:, ROWS:]
+
+    def hidden_back(m):
+        lp = flip_l(m)
         grad_act = dot_nt(cat_rows(GM, lp), WD[...].reshape(512, D))
-        grad_pre = (grad_act * slope).astype(BF16)
+        grad_pre = (grad_act * GA[m]).astype(BF16)
         GP[lp] = grad_pre[:ROWS]
         GP[4 + lp] = grad_pre[ROWS:]
         BG[0:1] += jnp.sum(grad_pre.astype(F32), axis=0, keepdims=True)
         scatter_m.emit(m, dot_nt(grad_pre, WI[...]))
 
     gather_n.sibling(0)
-    mlp(0)
+    hidden_part(0)
+    gather_n.forward(2)
     gather_n.forward(1)
-    gather_n.forward(2)
+    gather_g.forward(3)
+    gather_g.sibling(0)
+    spread_d.finish()
+    hidden_back(0)
+    gather_n.sibling(2)
+    hidden_part(1)
+    gather_g.sibling(2)
+    hidden_back(1)
     scatter_m.reduce(0)
     gather_n.sibling(1)
-    mlp(1)
+    hidden_part(2)
+    gather_g.sibling(1)
+    hidden_back(2)
     gather_n.forward(3)
-    gather_n.sibling(2)
-    mlp(2)
     scatter_m.reduce(1)
     gather_n.sibling(3)
-    mlp(3)
+    hidden_part(3)
+    gather_g.sibling(3)
     scatter_m.reduce(2)
+    hidden_back(3)
     scatter_m.reduce(3)
-    for k, m in enumerate((1, 2, 3, 0)):
-        scatter_b.emit(m, dot(HA[m], WD[...].reshape(512, D)))
-        if k:
-            scatter_b.reduce((1, 2, 3, 0)[k - 1])
-    scatter_b.reduce(0)
-    scatter_m.finish()
+
+    class Total:
+        def __init__(self, part, from_x, middle, from_z):
+            self.part, self.from_x, self.middle, self.from_z = part, from_x, middle, from_z
+            self.sem = slots(2)
+
+        def start(self):
+            half = pl.ds((1 - x) * 2, 2)
+            push(self.part.at[half], self.from_x, dev(dx=1), self.sem)
+
+        def second(self):
+            arrive(self.from_x, self.sem)
+            self.middle[...] = (
+                self.part[x * 2 + 1 - zh].astype(F32) + self.from_x[1 - zh].astype(F32)
+            ).astype(BF16)
+            push(self.middle, self.from_z, dev(dzh=1), self.sem + 1)
+
+        def result(self):
+            arrive(self.from_z, self.sem + 1)
+            return self.part[t].astype(F32) + self.from_x[zh].astype(F32) + self.from_z[...].astype(F32)
+
+    total_d = Total(GD, XD, HD, ZD)
+    total_i = Total(GI, XI, HI, ZI)
+    total_q = [Total(GQ.at[ch], XQ.at[ch], HQ.at[ch], ZQ.at[ch]) for ch in range(3)]
+    for ch in range(4):
+        GD[ch] = dot(HAT[ch * LANES : (ch + 1) * LANES, :], GM[...].reshape(8 * ROWS, D)).astype(BF16)
+    total_d.start()
+    all_pre = GP[...].reshape(8 * ROWS, 512)
+    for blk in range(8):
+        product = dot_tn(N2[:, :, blk * LANES : (blk + 1) * LANES].reshape(8 * ROWS, LANES), all_pre).astype(BF16)
+        for r in range(4):
+            tt, jj = shard_place(blk * 4 + r)
+            for ch in range(4):
+                GI[tt, jj, ch] = product[r * 32 : (r + 1) * 32, ch * LANES : (ch + 1) * LANES]
+    total_i.start()
 
     def norm_back(grad, normal, root, gain):
         scaled = grad * gain
         return root * (scaled - jnp.mean(scaled, axis=-1, keepdims=True)
                        - normal * jnp.mean(scaled * normal, axis=-1, keepdims=True))
 
+    scatter_m.finish()
     sums = [jnp.zeros((1, D), F32) for _ in range(4)]
     for r in range(4):
         rows = pl.ds(r * 32, 32)
@@ -892,67 +991,13 @@
             sums[i] += jnp.sum(value, axis=0, keepdims=True)
     vectors = {5: sums[0], 6: sums[1], 4: sums[2], 7: sums[3]}
     gather_b = Gather(GB)
-    gather_b.start()
-
-    class Total:
-        def __init__(self, part, from_x, middle, from_z):
-            self.part, self.from_x, self.middle, self.from_z = part, from_x, middle, from_z
-            self.sem = slots(2)
-
-        def start(self):
-            half = pl.ds((1 - x) * 2, 2)
-            push(self.part.at[half], self.from_x, dev(dx=1), self.sem)
-
-        def second(self):
-            arrive(self.from_x, self.sem)
-            self.middle[...] = (
-                self.part[x * 2 + 1 - zh].astype(F32) + self.from_x[1 - zh].astype(F32)
-            ).astype(BF16)
-            push(self.middle, self.from_z, dev(dzh=1), self.sem + 1)
-
-        def result(self):
-            arrive(self.from_z, self.sem + 1)
-            return self.part[t].astype(F32) + self.from_x[zh].astype(F32) + self.from_z[...].astype(F32)
-
-    total_d = Total(GD, XD, HD, ZD)
-    total_i = Total(GI, XI, HI, ZI)
-    total_q = Total(GQ, XQ, HQ, ZQ)
-    for ch in range(4):
-        GD[ch] = dot(HAT[ch * LANES : (ch + 1) * LANES, :], GM[...].reshape(8 * ROWS, D)).astype(BF16)
-    total_d.start()
-    gather_b.forward(1)
-    gather_b.forward(2)
-    all_pre = GP[...].reshape(8 * ROWS, 512)
-    for blk in range(8):
-        product = dot_tn(N2[:, :, blk * LANES : (blk + 1) * LANES].reshape(8 * ROWS, LANES), all_pre).astype(BF16)
-        for r in range(4):
-            i = blk * 4 + r
-            for ch in range(4):
-                GI[(i // 16) * 2 + (i // 4) % 2, ((i // 8) % 2) * 4 + i % 4, ch] = product[
-                    r * 32 : (r + 1) * 32, ch * LANES : (ch + 1) * LANES]
-    total_i.start()
-    gather_b.forward(3)
-
-    bias_d = PV[7:8, :]
-    sem_out, sem_in = slots(), slots()
-    scatter_b.finish()
-    for r in range(4):
-        rows = pl.ds(r * 32, 32)
-        CSB[0, rows] = (XO[rows] + scatter_b.rows(rows) + bias_d).astype(BF16)
-
-    @pl.when(native)
-    def _():
-        out_block[...] = CSB[0]
-
-    @pl.when(jnp.logical_not(native))
-    def _():
-        send(CSB.at[0], out_block, partner, sem_out)
+    gather_b.begin()
 
     DK[...] = jnp.zeros_like(DK)
     DV[...] = jnp.zeros_like(DV)
     GOF[...] = jnp.zeros_like(GOF)
-    for k, m in enumerate((0, 1, 2, 3)):
-        gather_b.sibling(m)
+
+    def attend_back(m):
         lp = flip_l(m)
         first, second = pair_lanes(lp)
         branch = cat_rows(GB, lp)
@@ -968,8 +1013,7 @@
             scaled_low_t = scaled_t.astype(BF16)
             scaled_low = scaled_t.T.astype(BF16)
             queries_h = only_lanes(queries, h).astype(BF16)
-
-            def back(i, carry):
+            for i in range(8):
                 rows = pl.ds(i * ROWS, ROWS)
                 probs = PT[m, h, rows]
                 value = dot(VV[rows], scaled_low_t)
@@ -977,94 +1021,66 @@
                 DV[rows] += dot(probs, scaled_low)
                 DK[rows] += dot(grad_scores, queries_h)
                 PT[m, h, rows] = grad_scores
-                return carry
-
-            for i in range(8):
-                back(i, 0)
             DQ[h * 64 : (h + 1) * 64, :] = dot(KT[h * 64 : (h + 1) * 64, :], PT[m, h]) * (HEAD_DIM ** -0.5)
         dq_rows = DQ[...].T.astype(BF16)
         GMX[lp, :, 0:LANES] = dq_rows[:ROWS]
         GMX[4 + lp, :, 0:LANES] = dq_rows[ROWS:]
-        if k == 0:
-            total_d.second()
-        if k == 2:
-            total_i.second()
-
-    GO[...] = GOF[...].astype(BF16)
-    sem_go, sem_gs = slots(4), slots(4)
-
-    @pl.when(jnp.logical_not(is_root))
-    def _():
-        send(GO, XGO.at[root_mask], (c * 2 + c, y * 4 + l), sem_go + root_mask)
+
+    def forward_out(m):
+        scatter_b.emit(m, dot(HA[m], WD[...].reshape(512, D)))
+
+    gather_b.sibling(0)
+    attend_back(0)
+    gather_b.forward(2)
+    gather_b.forward(1)
+    total_d.second()
+    gather_b.sibling(2)
+    attend_back(1)
+    gather_b.sibling(1)
+    attend_back(2)
+    gather_b.forward(3)
+    for m in attend_order:
+        forward_out(m)
+    total_i.second()
+    scatter_b.reduce(3)
+    gather_b.sibling(3)
+    attend_back(3)
+    scatter_b.reduce(1)
+    scatter_b.reduce(2)
+    scatter_b.reduce(0)
 
     for blk in range(8):
         rows = pl.ds(blk * ROWS, ROWS)
         GMX[blk, :, LANES : 2 * LANES] = DK[rows].astype(BF16)
         GMX[blk, :, 2 * LANES :] = DV[rows].astype(BF16)
-
+    all_mixed = GMX[...].reshape(8 * ROWS, 3 * LANES)
     scatter_n = Scatter(PA, CS, 3, scatter_m)
-    for k, m in enumerate(attend_order):
-        scatter_n.emit(m, dot_nt(cat_rows(GMX, flip_l(m)), WQ[...]))
-        if k:
-            scatter_n.reduce(attend_order[k - 1])
-    all_mixed = GMX[...].reshape(8 * ROWS, 3 * LANES)
+    scatter_n.emit(3, dot_nt(cat_rows(GMX, flip_l(3)), WQ[...]))
     for blk in range(8):
         product = dot_tn(N1[:, :, blk * LANES : (blk + 1) * LANES].reshape(8 * ROWS, LANES), all_mixed).astype(BF16)
         for r in range(4):
-            i = blk * 4 + r
+            tt, jj = shard_place(blk * 4 + r)
             for ch in range(3):
-                GQ[(i // 16) * 2 + (i // 4) % 2, ((i // 8) % 2) * 4 + i % 4, ch] = product[
-                    r * 32 : (r + 1) * 32, ch * LANES : (ch + 1) * LANES]
-        if blk == 1:
-            scatter_n.reduce(0)
-    total_q.start()
-
-    out_d[...] = total_d.result()
-    TI[...] = total_i.result().astype(BF16)
-    sem_ti, sem_tq = slots(8), slots(8)
-    for dc, dl in group_masks:
-        peer_j = flip(c, dc) * 4 + flip_l(dl)
-        push(TI.at[peer_j], RGI.at[j], dev(dc=dc, dl=dl), sem_ti + dc * 4 + dl)
-    RGI[j] = TI[j]
-
-    @pl.when(is_root)
-    def _():
-        total = GOF[...]
-        for mask in (1, 2, 3):
-            arrive(XGO.at[mask], sem_go + mask)
-            total += XGO[mask].astype(F32)
-        TGO[...] = total.astype(BF16).reshape(4, 32, D)
-        for slot in range(4):
-            mine = jnp.logical_and(zl == c, l == slot)
-
-            @pl.when(mine)
-            def _():
-                RGO[...] = TGO[slot]
-
-            @pl.when(jnp.logical_not(mine))
-            def _():
-                send(TGO.at[slot], RGO, (x * 2 + zl, zh * 4 + slot), sem_gs + slot)
-
-    scatter_n.finish()
+                GQ[ch, tt, jj] = product[r * 32 : (r + 1) * 32, ch * LANES : (ch + 1) * LANES]
+    scatter_n.reduce(3)
+    for ch in range(3):
+        total_q[ch].start()
+
+    for k, m in enumerate(attend_order):
+        if k:
+            scatter_n.emit(m, dot_nt(cat_rows(GMX, flip_l(m)), WQ[...]))
+        if k > 1:
+            scatter_n.reduce(attend_order[k - 1])
+    scatter_n.reduce(0)
+
     sums = [jnp.zeros((1, D), F32) for _ in range(2)]
-    for r in range(4):
-        rows = pl.ds(r * 32, 32)
-        grad = scatter_n.rows(rows)
-        normal, root, _ = norm_rows(X[j, rows].astype(F32), gain1, shift1)
-        XO[rows] = N2F[rows] + norm_back(grad, normal, root, gain1)
-        for i, value in enumerate((grad * normal, grad)):
-            sums[i] += jnp.sum(value, axis=0, keepdims=True)
+    for m in range(4):
+        lp = flip_l(m)
+        for half in range(2):
+            value = PA[m, half].astype(F32)
+            sums[0] += jnp.sum(value * N0[half * 4 + lp].astype(F32), axis=0, keepdims=True)
+            sums[1] += jnp.sum(value, axis=0, keepdims=True)
     vectors[0], vectors[1] = sums
-    left(CSB.at[1], scatter_b.far + 1)
-    CSB[1] = XO[...].astype(BF16)
-
-    @pl.when(native)
-    def _():
-        out_input[...] = CSB[1]
-
-    @pl.when(jnp.logical_not(native))
-    def _():
-        send(CSB.at[1], out_input, partner, sem_in)
 
     mixed_sums = jnp.sum(all_mixed.astype(F32), axis=0, keepdims=True)
     for q in range(8):
@@ -1082,13 +1098,28 @@
         mask = dx * 4 + dc * 2 + dzh
         push(VG.at[flip(x, dx) * 4 + flip(c, dc) * 2 + flip(zh, dzh)], VR.at[mask], dev(dx=dx, dc=dc, dzh=dzh), sem_v1 + mask)
 
-    total_q.second()
-    for dc, dl in group_masks:
-        arrive(RGI.at[flip(c, dc) * 4 + flip_l(dl)], sem_ti + dc * 4 + dl)
-    for jj in range(8):
-        for ch in range(4):
-            flat = (ch // 2) * 16 + (jj // 4) * 8 + (ch % 2) * 4 + jj % 4
-            out_i[:, flat * LANES : (flat + 1) * LANES] = RGI[jj, ch].astype(F32)
+    GO[...] = GOF[...].astype(BF16)
+    sem_go, sem_gs = slots(4), slots(4)
+
+    @pl.when(jnp.logical_not(is_root))
+    def _():
+        send(GO, XGO.at[root_mask], (c * 2 + c, y * 4 + l), sem_go + root_mask)
+
+    bias_d = PV[7:8, :]
+    sem_out, sem_in = slots(), slots()
+    scatter_b.finish()
+    for r in range(4):
+        rows = pl.ds(r * 32, 32)
+        BO[rows] = (XO[rows] + scatter_b.rows(rows) + bias_d).astype(BF16)
+    put_block = move(BO, out_block.at[0], 6)
+
+    @pl.when(native)
+    def _():
+        put_block.start()
+
+    @pl.when(foreign)
+    def _():
+        send(BO, out_block.at[0], partner, sem_out)
 
     slab = VG[q_own]
     for dx, dc, dzh in line_masks:
@@ -1099,52 +1130,118 @@
     for dl in (1, 2, 3):
         push(SL, SLR.at[dl], dev(dl=dl), sem_v2 + dl)
 
-    from_self = jnp.logical_and(x == c, l == pair_l)
-
-    @pl.when(jnp.logical_not(from_self))
-    def _():
-        arrive(RGO, sem_gs + l)
-
-    out_o[...] = RGO[...].astype(F32)
-
-    TQ[...] = total_q.result().astype(BF16)
+    TD[...] = total_d.result().astype(BF16)
+    put_d = move(TD, out_d, 7)
+    put_d.start()
+    TI[...] = total_i.result().astype(BF16)
+    sem_ti, sem_tq = slots(8), slots(8 * 3)
     for dc, dl in group_masks:
-        peer_j = flip(c, dc) * 4 + flip_l(dl)
-        push(TQ.at[peer_j], RGQ.at[j], dev(dc=dc, dl=dl), sem_tq + dc * 4 + dl)
-    RGQ[j] = TQ[j]
+        push(TI.at[group(dc, dl)], out_i.at[j], dev(dc=dc, dl=dl), sem_ti + dc * 4 + dl)
+    put_i = move(TI.at[j], out_i.at[j], 8)
+    put_i.start()
+
+    total_q[0].second()
+    total_q[1].second()
+
+    scatter_n.finish()
+    for r in range(4):
+        rows = pl.ds(r * 32, 32)
+        grad = scatter_n.rows(rows)
+        normal, root, _ = norm_rows(X[j, rows].astype(F32), gain1, shift1)
+        BI[rows] = (N2F[rows] + norm_back(grad, normal, root, gain1)).astype(BF16)
+    put_input = move(BI, out_input.at[0], 9)
+
+    @pl.when(native)
+    def _():
+        put_input.start()
+
+    @pl.when(foreign)
+    def _():
+        send(BI, out_input.at[0], partner, sem_in)
+
+    total_q[2].second()
+
+    put_o = move(TGO.at[l], out_o, 10)
+
+    @pl.when(is_root)
+    def _():
+        total = GOF[...]
+        for mask in (1, 2, 3):
+            arrive(XGO.at[mask], sem_go + mask)
+            total += XGO[mask].astype(F32)
+        TGO[...] = total.astype(BF16).reshape(4, 32, D)
+        for slot in range(4):
+            mine = jnp.logical_and(zl == c, l == slot)
+
+            @pl.when(mine)
+            def _():
+                put_o.start()
+
+            @pl.when(jnp.logical_not(mine))
+            def _():
+                send(TGO.at[slot], out_o, (x * 2 + zl, zh * 4 + slot), sem_gs + slot)
+
+    for ch in range(3):
+        TQ[ch] = total_q[ch].result().astype(BF16)
+        for dc, dl in group_masks:
+            push(TQ.at[ch, group(dc, dl)], out_q.at[ch, j], dev(dc=dc, dl=dl), sem_tq + ch * 8 + dc * 4 + dl)
+    put_q = [move(TQ.at[ch, j], out_q.at[ch, j], 11 + ch) for ch in range(3)]
+    for ch in range(3):
+        put_q[ch].start()
 
     for dl in (1, 2, 3):
         arrive(SLR.at[dl], sem_v2 + dl)
         slab += SLR[dl]
-    out_small[...] = slab
+    SLF[...] = slab
+    put_small = move(SLF, out_small, 14)
+    put_small.start()
 
     for dc, dl in group_masks:
-        arrive(RGQ.at[flip(c, dc) * 4 + flip_l(dl)], sem_tq + dc * 4 + dl)
-    for jj in range(8):
+        arrive(out_i.at[group(dc, dl)], sem_ti + dc * 4 + dl)
         for ch in range(3):
-            out_q[:, ch * D + jj * LANES : ch * D + (jj + 1) * LANES] = RGQ[jj, ch].astype(F32)
-
-    @pl.when(jnp.logical_not(native))
-    def _():
-        left(sgin, sem_ps)
-        left(xin, sem_px)
-        left(cin, sem_pc)
-        left(CSB.at[0], sem_out)
-        left(CSB.at[1], sem_in)
-        arrive(out_block, sem_out)
-        arrive(out_input, sem_in)
+            arrive(out_q.at[ch, group(dc, dl)], sem_tq + ch * 8 + dc * 4 + dl)
+
+    put_d.wait()
+    put_i.wait()
+    put_small.wait()
+    for ch in range(3):
+        put_q[ch].wait()
+
+    @pl.when(native)
+    def _():
+        put_block.wait()
+        put_input.wait()
+
+    @pl.when(foreign)
+    def _():
+        left(SGI, sem_ps)
+        left(xin.at[0], sem_px)
+        left(cin.at[0], sem_pc)
+        left(BO, sem_out)
+        left(BI, sem_in)
+        arrive(out_block.at[0], sem_out)
+        arrive(out_input.at[0], sem_in)
+
+    @pl.when(to_self)
+    def _():
+        put_o.wait()
 
     @pl.when(jnp.logical_not(to_self))
     def _():
         left(wo, sem_wo + l)
+        arrive(out_o, sem_gs + l)
 
     @pl.when(jnp.logical_not(is_root))
     def _():
         left(GO, sem_go + root_mask)
 
+    @pl.when(root_mask == 1)
+    def _():
+        left(WO, sem_wt + 3)
+
     @pl.when(is_root)
     def _():
-        for mask in (1, 2, 3):
+        for mask in (1, 2):
             left(WO, sem_wt + mask)
         for slot in range(4):
             @pl.when(jnp.logical_not(jnp.logical_and(zl == c, l == slot)))
@@ -1152,45 +1249,71 @@
                 left(TGO.at[slot], sem_gs + slot)
 
     scatter_n.close()
-    for m in range(4):
-        left(PB.at[m, 1 - c], scatter_b.near + m)
-        if m > 1:
-            left(CSB.at[m], scatter_b.far + m)
+    scatter_b.close()
+    for k in (1, 2):
+        left(X.at[j], gather_x.far + k)
+    left(X.at[j], gather_x.near)
     for copy in pending:
         copy.wait_send()
 
 
-def fused_scratch(copies):
-    def v(*shape, dtype=BF16):
-        return pltpu.VMEM(shape, dtype)
+def fused_scratch():
+    def v(*shape):
+        return pltpu.VMEM(shape, BF16)
 
     def f(*shape):
         return pltpu.VMEM(shape, F32)
 
     blocks = (8, ROWS, D)
     return [
-        v(*blocks), v(*blocks), v(*blocks), v(*blocks), v(*blocks),
-        f(8, 8, LANES), f(4, 16, LANES), f(8, 16, LANES), f(16, D),
-        v(8, 3, 32, LANES), v(4, 8, 3, 32, LANES), v(D, 3 * LANES), v(4, 32, D),
-        v(8, 4, 32, LANES), v(4, 8, 4, 32, LANES), v(D, 512), v(4, LANES, D),
+        v(*blocks), v(*blocks), v(*blocks), v(*blocks), v(*blocks), v(*blocks),
+        f(8, LANES), f(8, 8, LANES), f(16, LANES), f(4, 16, LANES), f(8, 16, LANES), f(16, D),
+        v(32, 3 * D), v(8, 3, 32, LANES), v(3, 4, 8, 32, LANES), v(D, 3 * LANES), v(4, 32, D),
+        v(32, 4 * D), v(8, 4, 32, LANES), v(4, 8, 4, 32, LANES), v(D, 512), v(4, LANES, D),
         v(D, LANES), v(D, LANES), v(D, LANES), v(LANES, D), v(LANES, D), v(LANES, D),
-        f(8, ROWS, LANES), f(D, 256), v(4, 2, D, 256), f(4, 2, 8, 256),
+        f(8, ROWS, LANES), f(2, D, 256), v(4, 2, D, 256), f(4, 2, 8, 256),
         f(4, LANES, 256), v(4, LANES, 256),
         v(4, 2, ROWS, D), v(4, ROWS, D), v(4, 2, ROWS, D), v(4, ROWS, D),
         v(4, 4, ROWS, D), v(4, 4, ROWS, D), f(ROWS, D), f(ROWS, D),
-        v(512, D), v(4, 256, 512), v(8, ROWS, 512),
+        v(512, D), v(4, 256, 512), v(8, ROWS, 512), f(4, 256, 512),
         f(D, LANES), f(D, LANES), f(LANES, 256), v(8, ROWS, 3 * LANES),
-        v(4, 8, 3, 32, LANES), v(4, 8, 4, 32, LANES), v(4, LANES, D),
-        v(2, 8, 3, 32, LANES), v(2, 8, 4, 32, LANES), v(2, LANES, D),
-        v(8, 3, 32, LANES), v(8, 4, 32, LANES), v(LANES, D),
-        v(8, 3, 32, LANES), v(8, 4, 32, LANES), v(LANES, D),
-        v(8, 3, 32, LANES), v(8, 4, 32, LANES),
-        v(8, 3, 32, LANES), v(8, 4, 32, LANES),
-        v(LANES, D), f(LANES, D), v(4, LANES, D), v(4, 32, D), v(32, D),
-        f(8, 16, LANES), f(8, 16, LANES), f(16, LANES), f(4, 16, LANES), f(ROWS, LANES), f(8, 512),
-        pltpu.SemaphoreType.DMA((copies,)),
-        pltpu.SemaphoreType.DMA((copies,)),
+        v(3, 4, 8, 32, LANES), v(4, 8, 4, 32, LANES), v(4, LANES, D),
+        v(3, 2, 8, 32, LANES), v(2, 8, 4, 32, LANES), v(2, LANES, D),
+        v(3, 8, 32, LANES), v(8, 4, 32, LANES), v(LANES, D),
+        v(3, 8, 32, LANES), v(8, 4, 32, LANES), v(LANES, D),
+        v(3, 8, 32, LANES), v(8, 4, 32, LANES), v(LANES, D),
+        v(LANES, D), f(LANES, D), v(4, LANES, D), v(4, 32, D),
+        f(8, 16, LANES), f(8, 16, LANES), f(16, LANES), f(4, 16, LANES), f(16, LANES),
+        f(ROWS, LANES), f(8, 512), v(ROWS, D), v(ROWS, D),
+        pltpu.SemaphoreType.DMA((COPIES,)),
+        pltpu.SemaphoreType.DMA((COPIES,)),
+        pltpu.SemaphoreType.DMA((16,)),
     ]
+
+
+def finish_kernel(
+    block, grad_in, grad_q, grad_o, grad_i, grad_d, small,
+    out_block, out_input, o0, o1, out_q, o2, o3, out_o, o4, o5, o6, out_i, ob, out_d, o7,
+):
+    place = lax.rem(lax.axis_index("band"), 4)
+    out_block[...] = block[...]
+    out_input[...] = grad_in[...]
+    for jj in range(8):
+        for ch in range(3):
+            out_q[:, ch * D + jj * LANES : ch * D + (jj + 1) * LANES] = grad_q[ch, jj].astype(F32)
+        for ch in range(4):
+            flat = flat_column(jj, ch)
+            out_i[:, flat * LANES : (flat + 1) * LANES] = grad_i[jj, ch].astype(F32)
+    out_o[...] = grad_o[...].astype(F32)
+    out_d[...] = grad_d[...].astype(F32)
+    slab = small[...]
+    mine = jnp.zeros((16, 32), F32)
+    for k in range(4):
+        mine = jnp.where(place == k, slab[:, k * 32 : (k + 1) * 32], mine)
+    for p, ref in enumerate((o0, o1, o2, o3, o4, o5, o6, o7)):
+        ref[...] = mine[p : p + 1].reshape(32)
+    pick = lax.broadcasted_iota(jnp.int32, (16, LANES), 0) == 8 + place
+    ob[...] = jnp.sum(jnp.where(pick, slab, 0.0), axis=0, keepdims=True).reshape(LANES)
 
 
 def fused_shards(
@@ -1212,55 +1335,46 @@
     segment_ids,
     sub_lengths,
 ):
-    place = lax.rem(lax.axis_index("band"), 4)
-    small = jnp.stack(
-        [
-            attention_norm_gain, attention_norm_bias, query_bias, value_bias,
-            output_bias, mlp_norm_gain, mlp_norm_bias, mlp_out_bias,
-        ]
-    ).astype(F32)
-    spread = (jnp.arange(LANES) // 32 == place)[None, :]
-    packed = jnp.concatenate(
-        [
-            jnp.where(spread, jnp.tile(small, (1, 4)), 0.0),
-            jnp.where((jnp.arange(8) == place)[:, None], mlp_in_bias.astype(F32)[None, :], 0.0),
-        ]
-    )
-    slots = jnp.concatenate(
-        [
-            segment_ids.astype(F32),
-            jnp.pad(sub_lengths.astype(F32), ((0, 6), (0, LANES - SUBGRIDS))),
-        ]
-    )
-    copies = 200
     vmem = pl.BlockSpec(memory_space=pltpu.VMEM)
-    block, grad_in, grad_q, grad_o, grad_i, grad_d, grad_small = pl.pallas_call(
-        functools.partial(fused_kernel, copies),
+    hbm = pl.BlockSpec(memory_space=pl.ANY)
+
+    def shape(dims, kind):
+        return jax.ShapeDtypeStruct(dims, kind)
+
+    parts = pl.pallas_call(
+        functools.partial(fused_kernel, COPIES),
         out_shape=(
-            jax.ShapeDtypeStruct((ROWS, D), BF16),
-            jax.ShapeDtypeStruct((ROWS, D), BF16),
-            jax.ShapeDtypeStruct((32, 3 * D), F32),
-            jax.ShapeDtypeStruct((32, D), F32),
-            jax.ShapeDtypeStruct((32, 4 * D), F32),
-            jax.ShapeDtypeStruct((LANES, D), F32),
-            jax.ShapeDtypeStruct((16, LANES), F32),
+            shape((1, ROWS, D), BF16),
+            shape((1, ROWS, D), BF16),
+            shape((3, 8, 32, LANES), BF16),
+            shape((32, D), BF16),
+            shape((8, 4, 32, LANES), BF16),
+            shape((LANES, D), BF16),
+            shape((16, LANES), F32),
         ),
-        in_specs=[vmem] * 8,
-        out_specs=(vmem,) * 7,
-        scratch_shapes=fused_scratch(copies),
+        in_specs=[hbm, hbm, vmem, vmem, hbm, hbm, hbm, hbm] + [vmem] * 9,
+        out_specs=(hbm,) * 7,
+        scratch_shapes=fused_scratch(),
         compiler_params=pltpu.CompilerParams(
             collective_id=0, has_side_effects=True, vmem_limit_bytes=63 * 2**20
         ),
     )(
-        block_in[0], cotangent[0], slots, packed,
+        block_in, cotangent, segment_ids, sub_lengths,
         query_key_value, output_weight, mlp_in_weight, mlp_out_weight,
-    )
-    mine = lax.dynamic_slice(grad_small, (0, place * 32), (8, 32))
-    grad_up_bias = lax.dynamic_index_in_dim(grad_small, 8 + place, 0, False)
-    return (
-        block[None], grad_in[None], mine[0], mine[1], grad_q, mine[2], mine[3], grad_o,
-        mine[4], mine[5], mine[6], grad_i, grad_up_bias, grad_d, mine[7],
-    )
+        attention_norm_gain, attention_norm_bias, query_bias, value_bias,
+        output_bias, mlp_norm_gain, mlp_norm_bias, mlp_out_bias, mlp_in_bias,
+    )
+    vector = shape((32,), F32)
+    return pl.pallas_call(
+        finish_kernel,
+        out_shape=(
+            shape((1, ROWS, D), BF16), shape((1, ROWS, D), BF16), vector, vector,
+            shape((32, 3 * D), F32), vector, vector, shape((32, D), F32), vector, vector, vector,
+            shape((32, 4 * D), F32), shape((LANES,), F32), shape((LANES, D), F32), vector,
+        ),
+        in_specs=[vmem] * 7,
+        out_specs=(vmem,) * 15,
+    )(*parts)
 
 
 def solution(mesh):

time: 228 us -> 182 us (0.80)
  Pallas kernels: 213 us -> 179 us
  local copies, waits for them, and re-layouts: 11.4 us -> 0 us
    pallas_call x1 -> x2, Pallas kernels: 213 us -> 179 us  [the longest x1 176 us: fused_shards(): pl.pallas_call(functools.partial(fused_kernel, COPIES), out_shape=(shape(...]
    unnamed x40 -> x0, local copies, waits for them, and re-layouts: 9.46 us -> none
where the time goes in v2:
time: 182 us; the launch traced here: 180 us
  Pallas kernels  179 us (98%)
    pallas_call x1, Pallas kernels, fused_shards(): pl.pallas_call(functools.partial(fused_kernel, COPIES), out_shape=(shape(...  176 us

profile of v2, /device:TPU:1, one launch (start us, length us, event | category | flops | bytes accessed | tf_op | source)
XLA Modules:
  0.0 179.9 jit_solution(3370115050725795397)
XLA Ops:
  0.7 176.2 %shard_map.280 = (bf16[1,128,1024]{2,1,0:T(8,128)(2,1)}, bf16[1,128,1024]{2,1,0:T(8,128)(2,1)}, bf16[3,8,32,128]{3,2,1,0:T(8,128)(2,1)}, bf16[32,1024]{1,0:T(8,1...) custom-call(bf16[1,128,1024]{2,1,0:T(8,128)(2,1)} %refs_0_.1, ...), custom_call_target="tpu_custom_call" | custom-call | tf_op jit(solution)/shard_map/pallas_call | solution.py:1344
  176.9 2.9 %shard_map.281 = (bf16[1,128,1024]{2,1,0:T(8,128)(2,1)}, bf16[1,128,1024]{2,1,0:T(8,128)(2,1)}, f32[32]{0:T(128)}, f32[32]{0:T(128)}, f32[32,3072]{1,0:T(8,128)}...) custom-call(bf16[1,128,1024]{2,1,0:T(8,128)(2,1)} %get-tuple-element, ...), custom_call_target="tpu_custom_call" | custom-call | tf_op jit(solution)/shard_map/pallas_call | solution.py:1368

commit v3 on v2

--- a/solution.py
+++ b/solution.py
@@ -591,10 +591,22 @@
         def __init__(self, buf):
             self.buf, self.sem = buf, slots(3)
 
+        def start_z(self, keep=True):
+            block = self.buf.at[t]
+            copy = send(block, block, dev(dzh=1), self.sem)
+            if keep:
+                pending.append(copy)
+
+        def start_x(self):
+            block = self.buf.at[t]
+            push(block, block, dev(dx=1), self.sem + 1)
+
+        def sent_z(self):
+            left(self.buf.at[t], self.sem)
+
         def start(self):
-            block = self.buf.at[t]
-            push(block, block, dev(dzh=1), self.sem)
-            push(block, block, dev(dx=1), self.sem + 1)
+            self.start_z()
+            self.start_x()
 
         def forward(self):
             block = self.buf.at[x * 2 + 1 - zh]
@@ -638,6 +650,10 @@
         send(WO, WO, dev(dzh=1), sem_wt + 1)
         send(WO, WO, dev(dx=1), sem_wt + 2)
 
+
+    @pl.when(foreign)
+    def _():
+        send(cin.at[0], GM.at[their_block], partner, sem_pc)
 
     for dx, dc, dzh in line_masks:
         arrive(FULL.at[flip(x, dx) * 4 + flip(c, dc) * 2 + flip(zh, dzh)], sem_s2 + dx * 4 + dc * 2 + dzh)
@@ -668,6 +684,15 @@
     norm_one(c * 4 + roles[1])
     norm_one(c * 4 + roles[2])
     spread_q[0].forward()
+    get_i.wait()
+    for jj in range(8):
+        for ch in range(4):
+            flat = flat_column(jj, ch)
+            WSI[jj, ch] = WII[:, flat * LANES : (flat + 1) * LANES]
+    sem_wi = slots(8)
+    for dc, dl in group_masks:
+        push(WSI.at[group(dc, dl)], RI.at[t, j], dev(dc=dc, dl=dl), sem_wi + dc * 4 + dl)
+    RI[t, j] = WSI[j]
     for k in (1, 2):
         gather_x.sibling(k)
     gather_x.forward(3)
@@ -679,19 +704,6 @@
     gather_x.sibling(3)
     norm_one((1 - c) * 4 + roles[3])
 
-    @pl.when(foreign)
-    def _():
-        send(cin.at[0], GM.at[their_block], partner, sem_pc)
-
-    get_i.wait()
-    for jj in range(8):
-        for ch in range(4):
-            flat = flat_column(jj, ch)
-            WSI[jj, ch] = WII[:, flat * LANES : (flat + 1) * LANES]
-    sem_wi = slots(8)
-    for dc, dl in group_masks:
-        push(WSI.at[group(dc, dl)], RI.at[t, j], dev(dc=dc, dl=dl), sem_wi + dc * 4 + dl)
-    RI[t, j] = WSI[j]
     get_d.wait()
     spread_i, spread_d = Spread(RI), Spread(WD)
 
@@ -713,6 +725,18 @@
         ident = jnp.sum(label_row * onehot, axis=1, keepdims=True)
         CODE[blk] = jnp.broadcast_to(jnp.where(rank < limit, ident, -1.0), (ROWS, LANES))
 
+    @pl.when(native)
+    def _():
+        get_c.wait()
+
+    @pl.when(foreign)
+    def _():
+        arrive(GM.at[j], sem_pc)
+
+    is_real = CODE[j][:, 0:1] >= 0.0
+    GM[j] = jnp.where(is_real, GM[j].astype(F32), 0.0).astype(BF16)
+    gather_g.begin()
+
     @pl.when(jnp.logical_not(is_root))
     def _():
         arrive(WO, sem_wt + root_mask)
@@ -721,6 +745,11 @@
     def _():
         send(WO, WO, dev(dx=1), sem_wt + 3)
 
+    for dc, dl in group_masks:
+        arrive(RI.at[t, group(dc, dl)], sem_wi + dc * 4 + dl)
+    spread_i.start_z()
+    spread_i.start_x()
+    spread_d.start_x()
     for ch in range(3):
         spread_q[ch].finish()
         for i in range(32):
@@ -741,22 +770,6 @@
         KT[:, rows] = keys.T.astype(BF16)
         VT[:, rows] = values.T.astype(BF16)
 
-    for dc, dl in group_masks:
-        arrive(RI.at[t, group(dc, dl)], sem_wi + dc * 4 + dl)
-    spread_i.start()
-    spread_d.start()
-
-    @pl.when(native)
-    def _():
-        get_c.wait()
-
-    @pl.when(foreign)
-    def _():
-        arrive(GM.at[j], sem_pc)
-
-    is_real = CODE[j][:, 0:1] >= 0.0
-    GM[j] = jnp.where(is_real, GM[j].astype(F32), 0.0).astype(BF16)
-    gather_g.begin()
 
     def pair_lanes(lp):
         return (pl.ds(pl.multiple_of(lp * LANES, LANES), LANES), pl.ds(pl.multiple_of(512 + lp * LANES, LANES), LANES))
@@ -771,7 +784,7 @@
     class Scatter:
         def __init__(self, part, chip, number, before=None, tree=True):
             self.part, self.chip, self.number, self.before, self.tree = part, chip, number, before, tree
-            self.near, self.far = slots(4), slots(4)
+            self.near, self.far = slots(4), slots(8)
 
         def emit(self, m, value):
             if self.before is not None:
@@ -781,23 +794,35 @@
             self.part[m, 1] = low[ROWS:]
             send(self.part.at[m, 1 - c], SB.at[self.number, m], dev(dc=1), self.near + m)
 
+        def pieces(self, m):
+            if self.tree and m > 1:
+                return ((pl.ds(0, 64), self.far + m), (pl.ds(64, 64), self.far + 4 + m))
+            return ((pl.ds(0, ROWS), self.far + m),)
+
+        def chip_left(self, m):
+            for rows, sem in self.pieces(m):
+                left(self.chip.at[m, rows], sem)
+
         def reduce(self, m):
             arrive(SB.at[self.number, m], self.near + m)
             if m == 0:
                 return
             if self.before is not None:
-                left(self.chip.at[m], self.before.far + m)
-            total = self.part[m, c].astype(F32) + SB[self.number, m].astype(F32)
-            if self.tree and m == 2:
-                arrive(RV.at[self.number, 3], self.far + 3)
-                total += RV[self.number, 3].astype(F32)
-            self.chip[m] = total.astype(BF16)
-            device = dev(dl=1) if self.tree and m == 3 else dev(dl=m)
-            send(self.chip.at[m], RV.at[self.number, m], device, self.far + m)
+                self.before.chip_left(m)
+            for k, (rows, sem) in enumerate(self.pieces(m)):
+                total = self.part[m, c, rows].astype(F32) + SB[self.number, m, rows].astype(F32)
+                if self.tree and m == 2:
+                    across = RV.at[self.number, 3, rows]
+                    arrive(across, self.pieces(3)[k][1])
+                    total += across[...].astype(F32)
+                self.chip[m, rows] = total.astype(BF16)
+                device = dev(dl=1) if self.tree and m == 3 else dev(dl=m)
+                send(self.chip.at[m, rows], RV.at[self.number, m, rows], device, sem)
 
         def finish(self):
             for m in (1, 2) if self.tree else (1, 2, 3):
-                arrive(RV.at[self.number, m], self.far + m)
+                for rows, sem in self.pieces(m):
+                    arrive(RV.at[self.number, m, rows], sem)
 
         def rows(self, rows):
             total = self.part[0, c, rows].astype(F32) + SB[self.number, 0, rows].astype(F32)
@@ -809,7 +834,7 @@
             for m in range(4):
                 left(self.part.at[m, 1 - c], self.near + m)
                 if m:
-                    left(self.chip.at[m], self.far + m)
+                    self.chip_left(m)
 
     head_rows = lax.broadcasted_iota(jnp.int32, (LANES, 256), 0)
     head_lanes = lax.broadcasted_iota(jnp.int32, (256, LANES), 1)
@@ -849,6 +874,12 @@
             OT[m, h * 64 : (h + 1) * 64] = dot(VT[h * 64 : (h + 1) * 64, :], PT[m, h]) * inverse
             if k and h == 0:
                 scatter_a.reduce(attend_order[k - 1])
+            if k == 1 and h == 1:
+                spread_d.start_z()
+            if k == 2 and h == 0:
+                gather_g.forward(2)
+            if k == 3 and h == 1:
+                gather_g.forward(1)
         joined = OT[m]
         OL[m] = joined.astype(BF16)
         scatter_a.emit(m, dot(joined.T.astype(BF16), WO[...].reshape(LANES, D)))
@@ -868,9 +899,6 @@
     gather_n = Gather(N2)
     gather_n.begin()
 
-    for k in (1, 2):
-        gather_g.forward(k)
-    spread_d.forward()
     spread_i.finish()
     for i in range(32):
         tt, jj = shard_place(i)
@@ -912,6 +940,7 @@
 
     gather_n.sibling(0)
     hidden_part(0)
+    spread_d.forward()
     gather_n.forward(2)
     gather_n.forward(1)
     gather_g.forward(3)
@@ -939,20 +968,23 @@
     class Total:
         def __init__(self, part, from_x, middle, from_z):
             self.part, self.from_x, self.middle, self.from_z = part, from_x, middle, from_z
-            self.sem = slots(2)
-
-        def start(self):
-            half = pl.ds((1 - x) * 2, 2)
-            push(self.part.at[half], self.from_x, dev(dx=1), self.sem)
+            self.sem = slots(3)
+
+        def start_cross(self):
+            push(self.part.at[(1 - x) * 2 + 1 - zh], self.from_x.at[1 - zh], dev(dx=1), self.sem)
+
+        def start_keep(self):
+            push(self.part.at[(1 - x) * 2 + zh], self.from_x.at[zh], dev(dx=1), self.sem + 2)
 
         def second(self):
-            arrive(self.from_x, self.sem)
+            arrive(self.from_x.at[1 - zh], self.sem)
             self.middle[...] = (
                 self.part[x * 2 + 1 - zh].astype(F32) + self.from_x[1 - zh].astype(F32)
             ).astype(BF16)
             push(self.middle, self.from_z, dev(dzh=1), self.sem + 1)
 
         def result(self):
+            arrive(self.from_x.at[zh], self.sem + 2)
             arrive(self.from_z, self.sem + 1)
             return self.part[t].astype(F32) + self.from_x[zh].astype(F32) + self.from_z[...].astype(F32)
 
@@ -961,7 +993,7 @@
     total_q = [Total(GQ.at[ch], XQ.at[ch], HQ.at[ch], ZQ.at[ch]) for ch in range(3)]
     for ch in range(4):
         GD[ch] = dot(HAT[ch * LANES : (ch + 1) * LANES, :], GM[...].reshape(8 * ROWS, D)).astype(BF16)
-    total_d.start()
+    total_d.start_cross()
     all_pre = GP[...].reshape(8 * ROWS, 512)
     for blk in range(8):
         product = dot_tn(N2[:, :, blk * LANES : (blk + 1) * LANES].reshape(8 * ROWS, LANES), all_pre).astype(BF16)
@@ -969,13 +1001,20 @@
             tt, jj = shard_place(blk * 4 + r)
             for ch in range(4):
                 GI[tt, jj, ch] = product[r * 32 : (r + 1) * 32, ch * LANES : (ch + 1) * LANES]
-    total_i.start()
+    total_i.start_cross()
+    total_d.start_keep()
+    total_i.start_keep()
 
     def norm_back(grad, normal, root, gain):
         scaled = grad * gain
         return root * (scaled - jnp.mean(scaled, axis=-1, keepdims=True)
                        - normal * jnp.mean(scaled * normal, axis=-1, keepdims=True))
 
+    def forward_out(m):
+        scatter_b.emit(m, dot(HA[m], WD[...].reshape(512, D)))
+
+    for m in attend_order:
+        forward_out(m)
     scatter_m.finish()
     sums = [jnp.zeros((1, D), F32) for _ in range(4)]
     for r in range(4):
@@ -1026,28 +1065,23 @@
         GMX[lp, :, 0:LANES] = dq_rows[:ROWS]
         GMX[4 + lp, :, 0:LANES] = dq_rows[ROWS:]
 
-    def forward_out(m):
-        scatter_b.emit(m, dot(HA[m], WD[...].reshape(512, D)))
-
+    total_d.second()
     gather_b.sibling(0)
     attend_back(0)
     gather_b.forward(2)
     gather_b.forward(1)
-    total_d.second()
+    scatter_b.reduce(3)
     gather_b.sibling(2)
     attend_back(1)
+    total_i.second()
     gather_b.sibling(1)
     attend_back(2)
     gather_b.forward(3)
-    for m in attend_order:
-        forward_out(m)
-    total_i.second()
-    scatter_b.reduce(3)
+    scatter_b.reduce(1)
+    scatter_b.reduce(0)
     gather_b.sibling(3)
     attend_back(3)
-    scatter_b.reduce(1)
     scatter_b.reduce(2)
-    scatter_b.reduce(0)
 
     for blk in range(8):
         rows = pl.ds(blk * ROWS, ROWS)
@@ -1055,22 +1089,39 @@
         GMX[blk, :, 2 * LANES :] = DV[rows].astype(BF16)
     all_mixed = GMX[...].reshape(8 * ROWS, 3 * LANES)
     scatter_n = Scatter(PA, CS, 3, scatter_m)
-    scatter_n.emit(3, dot_nt(cat_rows(GMX, flip_l(3)), WQ[...]))
-    for blk in range(8):
+
+    def back_out(m):
+        scatter_n.emit(m, dot_nt(cat_rows(GMX, flip_l(m)), WQ[...]))
+
+    def joint_grad(blk):
         product = dot_tn(N1[:, :, blk * LANES : (blk + 1) * LANES].reshape(8 * ROWS, LANES), all_mixed).astype(BF16)
         for r in range(4):
             tt, jj = shard_place(blk * 4 + r)
             for ch in range(3):
                 GQ[ch, tt, jj] = product[r * 32 : (r + 1) * 32, ch * LANES : (ch + 1) * LANES]
+
+    back_out(3)
+    for blk in range(4):
+        joint_grad(blk)
     scatter_n.reduce(3)
+    for blk in range(4, 8):
+        joint_grad(blk)
     for ch in range(3):
-        total_q[ch].start()
-
-    for k, m in enumerate(attend_order):
-        if k:
-            scatter_n.emit(m, dot_nt(cat_rows(GMX, flip_l(m)), WQ[...]))
-        if k > 1:
-            scatter_n.reduce(attend_order[k - 1])
+        total_q[ch].start_cross()
+    for ch in range(3):
+        total_q[ch].start_keep()
+
+    back_out(1)
+    back_out(2)
+    scatter_n.reduce(1)
+    back_out(0)
+    GO[...] = GOF[...].astype(BF16)
+    sem_go, sem_gs = slots(4), slots(4)
+
+    @pl.when(jnp.logical_not(is_root))
+    def _():
+        send(GO, XGO.at[root_mask], (c * 2 + c, y * 4 + l), sem_go + root_mask)
+
     scatter_n.reduce(0)
 
     sums = [jnp.zeros((1, D), F32) for _ in range(2)]
@@ -1081,7 +1132,7 @@
             sums[0] += jnp.sum(value * N0[half * 4 + lp].astype(F32), axis=0, keepdims=True)
             sums[1] += jnp.sum(value, axis=0, keepdims=True)
     vectors[0], vectors[1] = sums
-
+    scatter_n.reduce(2)
     mixed_sums = jnp.sum(all_mixed.astype(F32), axis=0, keepdims=True)
     for q in range(8):
         VG[q] = jnp.zeros((16, LANES), F32)
@@ -1098,12 +1149,8 @@
         mask = dx * 4 + dc * 2 + dzh
         push(VG.at[flip(x, dx) * 4 + flip(c, dc) * 2 + flip(zh, dzh)], VR.at[mask], dev(dx=dx, dc=dc, dzh=dzh), sem_v1 + mask)
 
-    GO[...] = GOF[...].astype(BF16)
-    sem_go, sem_gs = slots(4), slots(4)
-
-    @pl.when(jnp.logical_not(is_root))
-    def _():
-        send(GO, XGO.at[root_mask], (c * 2 + c, y * 4 + l), sem_go + root_mask)
+    for ch in range(3):
+        total_q[ch].second()
 
     bias_d = PV[7:8, :]
     sem_out, sem_in = slots(), slots()
@@ -1120,6 +1167,22 @@
     @pl.when(foreign)
     def _():
         send(BO, out_block.at[0], partner, sem_out)
+
+    scatter_n.finish()
+    for r in range(4):
+        rows = pl.ds(r * 32, 32)
+        grad = scatter_n.rows(rows)
+        normal, root, _ = norm_rows(X[j, rows].astype(F32), gain1, shift1)
+        BI[rows] = (N2F[rows] + norm_back(grad, normal, root, gain1)).astype(BF16)
+    put_input = move(BI, out_input.at[0], 9)
+
+    @pl.when(native)
+    def _():
+        put_input.start()
+
+    @pl.when(foreign)
+    def _():
+        send(BI, out_input.at[0], partner, sem_in)
 
     slab = VG[q_own]
     for dx, dc, dzh in line_masks:
@@ -1139,27 +1202,6 @@
         push(TI.at[group(dc, dl)], out_i.at[j], dev(dc=dc, dl=dl), sem_ti + dc * 4 + dl)
     put_i = move(TI.at[j], out_i.at[j], 8)
     put_i.start()
-
-    total_q[0].second()
-    total_q[1].second()
-
-    scatter_n.finish()
-    for r in range(4):
-        rows = pl.ds(r * 32, 32)
-        grad = scatter_n.rows(rows)
-        normal, root, _ = norm_rows(X[j, rows].astype(F32), gain1, shift1)
-        BI[rows] = (N2F[rows] + norm_back(grad, normal, root, gain1)).astype(BF16)
-    put_input = move(BI, out_input.at[0], 9)
-
-    @pl.when(native)
-    def _():
-        put_input.start()
-
-    @pl.when(foreign)
-    def _():
-        send(BI, out_input.at[0], partner, sem_in)
-
-    total_q[2].second()
 
     put_o = move(TGO.at[l], out_o, 10)
 

time: 182 us -> 166 us (0.912)
  Pallas kernels: 179 us -> 165 us
    pallas_call x1, Pallas kernels: 176 us -> 162 us  [fused_shards(): pl.pallas_call(functools.partial(fused_kernel, COPIES), out_shape=(shape(...]
where the time goes in v3:
time: 166 us; the launch traced here: 165 us
  Pallas kernels  165 us (99%)
    pallas_call x1, Pallas kernels, fused_shards(): pl.pallas_call(functools.partial(fused_kernel, COPIES), out_shape=(shape(...  162 us

profile of v3, /device:TPU:1, one launch (start us, length us, event | category | flops | bytes accessed | tf_op | source)
XLA Modules:
  0.0 165.4 jit_solution(5964010654140089121)
XLA Ops:
  0.7 161.7 %shard_map.280 = (bf16[1,128,1024]{2,1,0:T(8,128)(2,1)}, bf16[1,128,1024]{2,1,0:T(8,128)(2,1)}, bf16[3,8,32,128]{3,2,1,0:T(8,128)(2,1)}, bf16[32,1024]{1,0:T(8,1...) custom-call(bf16[1,128,1024]{2,1,0:T(8,128)(2,1)} %refs_0_.1, ...), custom_call_target="tpu_custom_call" | custom-call | tf_op jit(solution)/shard_map/pallas_call | solution.py:1386
  162.4 2.9 %shard_map.281 = (bf16[1,128,1024]{2,1,0:T(8,128)(2,1)}, bf16[1,128,1024]{2,1,0:T(8,128)(2,1)}, f32[32]{0:T(128)}, f32[32]{0:T(128)}, f32[32,3072]{1,0:T(8,128)}...) custom-call(bf16[1,128,1024]{2,1,0:T(8,128)(2,1)} %get-tuple-element, ...), custom_call_target="tpu_custom_call" | custom-call | tf_op jit(solution)/shard_map/pallas_call | solution.py:1410

commit v4 on v3

--- a/solution.py
+++ b/solution.py
@@ -390,6 +390,10 @@
     return lax.dot_general(lhs, rhs, (((0,), (0,)), ((), ())), preferred_element_type=F32)
 
 
+def pair_of(jj):
+    return (jj // 4) * 4 + (jj % 2) * 2 + (jj // 2) % 2
+
+
 def flat_column(jj, ch):
     return (ch // 2) * 16 + (jj // 4) * 8 + (ch % 2) * 4 + jj % 4
 
@@ -506,7 +510,7 @@
     get_q.wait()
     for jj in range(8):
         for ch in range(3):
-            WSQ[jj, ch] = WQI[:, ch * D + jj * LANES : ch * D + (jj + 1) * LANES]
+            WSQ[jj, ch] = WQI[:, ch * D + pair_of(jj) * LANES : ch * D + (pair_of(jj) + 1) * LANES]
     for ch in range(3):
         RQ[ch, t, j] = WSQ[j, ch]
     pl.semaphore_wait(barrier, len(peers))
@@ -563,10 +567,11 @@
         gather_x.start()
 
     sem_wo, sem_wt = slots(4), slots(4)
-    pair_l = c * 2 + zh
+    own_pair = c * 4 + y * 2 + zl
+    pair_l = zh * 2 + c
     to_self = jnp.logical_and(x == c, l == pair_l)
-    is_root = jnp.logical_and(x == c, zh == y)
-    root_mask = jnp.abs(x - c) * 2 + jnp.abs(zh - y)
+    is_root = jnp.logical_and(x == c, zh == zl)
+    root_mask = jnp.abs(x - c) * 2 + jnp.abs(zh - zl)
     get_o = move(wo, WO.at[l], 5)
 
     @pl.when(to_self)
@@ -637,7 +642,7 @@
         gather_x.start()
 
     for slot in range(4):
-        @pl.when(jnp.logical_and(is_root, jnp.logical_not(jnp.logical_and(zl == c, l == slot))))
+        @pl.when(jnp.logical_and(is_root, jnp.logical_not(jnp.logical_and(y == c, l == slot))))
         def _():
             arrive(WO.at[slot], sem_wo + slot)
 
@@ -755,7 +760,7 @@
         for i in range(32):
             tt, jj = shard_place(i)
             WQ[i * 32 : (i + 1) * 32, ch * LANES : (ch + 1) * LANES] = RQ[ch, tt, jj]
-    bias_q, bias_v = FULL[j][2:3, :], FULL[j][3:4, :]
+    bias_q, bias_v = FULL[own_pair][2:3, :], FULL[own_pair][3:4, :]
     for k in range(4):
         rows = pl.ds(k * 256, 256)
         normed = N1[2 * k : 2 * k + 2].reshape(256, D)
@@ -1100,27 +1105,25 @@
             for ch in range(3):
                 GQ[ch, tt, jj] = product[r * 32 : (r + 1) * 32, ch * LANES : (ch + 1) * LANES]
 
-    back_out(3)
-    for blk in range(4):
-        joint_grad(blk)
-    scatter_n.reduce(3)
-    for blk in range(4, 8):
+    for blk in range(8):
         joint_grad(blk)
     for ch in range(3):
         total_q[ch].start_cross()
     for ch in range(3):
         total_q[ch].start_keep()
 
+    back_out(3)
     back_out(1)
+    scatter_n.reduce(3)
     back_out(2)
     scatter_n.reduce(1)
     back_out(0)
     GO[...] = GOF[...].astype(BF16)
     sem_go, sem_gs = slots(4), slots(4)
 
-    @pl.when(jnp.logical_not(is_root))
-    def _():
-        send(GO, XGO.at[root_mask], (c * 2 + c, y * 4 + l), sem_go + root_mask)
+    @pl.when(x != c)
+    def _():
+        send(GO, XGO.at[0], dev(dx=1), sem_go)
 
     scatter_n.reduce(0)
 
@@ -1139,7 +1142,7 @@
         for p in (0, 1, 4, 5, 6, 7):
             VG[q, p : p + 1] = vectors[p][:, q * LANES : (q + 1) * LANES]
         for p, ch in ((2, 0), (3, 2)):
-            VG[q, p : p + 1] = jnp.where(j == q, mixed_sums[:, ch * LANES : (ch + 1) * LANES], 0.0)
+            VG[q, p : p + 1] = jnp.where(own_pair == q, mixed_sums[:, ch * LANES : (ch + 1) * LANES], 0.0)
         ch = (q // 4) * 2 + q % 2
         for r in range(4):
             here = jnp.logical_and(c == (q // 2) % 2, l == r)
@@ -1149,6 +1152,16 @@
         mask = dx * 4 + dc * 2 + dzh
         push(VG.at[flip(x, dx) * 4 + flip(c, dc) * 2 + flip(zh, dzh)], VR.at[mask], dev(dx=dx, dc=dc, dzh=dzh), sem_v1 + mask)
 
+    @pl.when(x == c)
+    def _():
+        arrive(XGO.at[0], sem_go)
+        GOF[...] += XGO[0].astype(F32)
+
+    @pl.when(root_mask == 1)
+    def _():
+        GO[...] = GOF[...].astype(BF16)
+        send(GO, XGO.at[1], dev(dzh=1), sem_go + 1)
+
     for ch in range(3):
         total_q[ch].second()
 
@@ -1167,31 +1180,6 @@
     @pl.when(foreign)
     def _():
         send(BO, out_block.at[0], partner, sem_out)
-
-    scatter_n.finish()
-    for r in range(4):
-        rows = pl.ds(r * 32, 32)
-        grad = scatter_n.rows(rows)
-        normal, root, _ = norm_rows(X[j, rows].astype(F32), gain1, shift1)
-        BI[rows] = (N2F[rows] + norm_back(grad, normal, root, gain1)).astype(BF16)
-    put_input = move(BI, out_input.at[0], 9)
-
-    @pl.when(native)
-    def _():
-        put_input.start()
-
-    @pl.when(foreign)
-    def _():
-        send(BI, out_input.at[0], partner, sem_in)
-
-    slab = VG[q_own]
-    for dx, dc, dzh in line_masks:
-        mask = dx * 4 + dc * 2 + dzh
-        arrive(VR.at[mask], sem_v1 + mask)
-        slab += VR[mask]
-    SL[...] = slab
-    for dl in (1, 2, 3):
-        push(SL, SLR.at[dl], dev(dl=dl), sem_v2 + dl)
 
     TD[...] = total_d.result().astype(BF16)
     put_d = move(TD, out_d, 7)
@@ -1203,17 +1191,23 @@
     put_i = move(TI.at[j], out_i.at[j], 8)
     put_i.start()
 
+    slab = VG[q_own]
+    for dx, dc, dzh in line_masks:
+        mask = dx * 4 + dc * 2 + dzh
+        arrive(VR.at[mask], sem_v1 + mask)
+        slab += VR[mask]
+    SL[...] = slab
+    for dl in (1, 2, 3):
+        push(SL, SLR.at[dl], dev(dl=dl), sem_v2 + dl)
+
     put_o = move(TGO.at[l], out_o, 10)
 
     @pl.when(is_root)
     def _():
-        total = GOF[...]
-        for mask in (1, 2, 3):
-            arrive(XGO.at[mask], sem_go + mask)
-            total += XGO[mask].astype(F32)
-        TGO[...] = total.astype(BF16).reshape(4, 32, D)
+        arrive(XGO.at[1], sem_go + 1)
+        TGO[...] = (GOF[...] + XGO[1].astype(F32)).astype(BF16).reshape(4, 32, D)
         for slot in range(4):
-            mine = jnp.logical_and(zl == c, l == slot)
+            mine = jnp.logical_and(y == c, l == slot)
 
             @pl.when(mine)
             def _():
@@ -1221,7 +1215,23 @@
 
             @pl.when(jnp.logical_not(mine))
             def _():
-                send(TGO.at[slot], out_o, (x * 2 + zl, zh * 4 + slot), sem_gs + slot)
+                send(TGO.at[slot], out_o, (x * 2 + y, zh * 4 + slot), sem_gs + slot)
+
+    scatter_n.finish()
+    for r in range(4):
+        rows = pl.ds(r * 32, 32)
+        grad = scatter_n.rows(rows)
+        normal, root, _ = norm_rows(X[j, rows].astype(F32), gain1, shift1)
+        BI[rows] = (N2F[rows] + norm_back(grad, normal, root, gain1)).astype(BF16)
+    put_input = move(BI, out_input.at[0], 9)
+
+    @pl.when(native)
+    def _():
+        put_input.start()
+
+    @pl.when(foreign)
+    def _():
+        send(BI, out_input.at[0], partner, sem_in)
 
     for ch in range(3):
         TQ[ch] = total_q[ch].result().astype(BF16)
@@ -1273,9 +1283,13 @@
         left(wo, sem_wo + l)
         arrive(out_o, sem_gs + l)
 
-    @pl.when(jnp.logical_not(is_root))
-    def _():
-        left(GO, sem_go + root_mask)
+    @pl.when(x != c)
+    def _():
+        left(GO, sem_go)
+
+    @pl.when(root_mask == 1)
+    def _():
+        left(GO, sem_go + 1)
 
     @pl.when(root_mask == 1)
     def _():
@@ -1286,7 +1300,7 @@
         for mask in (1, 2):
             left(WO, sem_wt + mask)
         for slot in range(4):
-            @pl.when(jnp.logical_not(jnp.logical_and(zl == c, l == slot)))
+            @pl.when(jnp.logical_not(jnp.logical_and(y == c, l == slot)))
             def _():
                 left(TGO.at[slot], sem_gs + slot)
 
@@ -1342,7 +1356,7 @@
     out_input[...] = grad_in[...]
     for jj in range(8):
         for ch in range(3):
-            out_q[:, ch * D + jj * LANES : ch * D + (jj + 1) * LANES] = grad_q[ch, jj].astype(F32)
+            out_q[:, ch * D + pair_of(jj) * LANES : ch * D + (pair_of(jj) + 1) * LANES] = grad_q[ch, jj].astype(F32)
         for ch in range(4):
             flat = flat_column(jj, ch)
             out_i[:, flat * LANES : (flat + 1) * LANES] = grad_i[jj, ch].astype(F32)

time: 166 us -> 161 us (0.970)
  Pallas kernels: 165 us -> 160 us
    pallas_call x1, Pallas kernels: 162 us -> 157 us  [fused_shards(): pl.pallas_call(functools.partial(fused_kernel, COPIES), out_shape=(shape(...]
where the time goes in v4:
time: 161 us
  Pallas kernels  160 us (99%)
    pallas_call x1, Pallas kernels, fused_shards(): pl.pallas_call(functools.partial(fused_kernel, COPIES), out_shape=(shape(...  157 us

profile of v4, /device:TPU:1, one launch (start us, length us, event | category | flops | bytes accessed | tf_op | source)
XLA Modules:
  0.0 160.6 jit_solution(13765906599913854686)
XLA Ops:
  0.7 156.9 %shard_map.280 = (bf16[1,128,1024]{2,1,0:T(8,128)(2,1)}, bf16[1,128,1024]{2,1,0:T(8,128)(2,1)}, bf16[3,8,32,128]{3,2,1,0:T(8,128)(2,1)}, bf16[32,1024]{1,0:T(8,1...) custom-call(bf16[1,128,1024]{2,1,0:T(8,128)(2,1)} %refs_0_.1, ...), custom_call_target="tpu_custom_call" | custom-call | tf_op jit(solution)/shard_map/pallas_call | solution.py:1400
  157.5 2.9 %shard_map.281 = (bf16[1,128,1024]{2,1,0:T(8,128)(2,1)}, bf16[1,128,1024]{2,1,0:T(8,128)(2,1)}, f32[32]{0:T(128)}, f32[32]{0:T(128)}, f32[32,3072]{1,0:T(8,128)}...) custom-call(bf16[1,128,1024]{2,1,0:T(8,128)(2,1)} %get-tuple-element, ...), custom_call_target="tpu_custom_call" | custom-call | tf_op jit(solution)/shard_map/pallas_call | solution.py:1424

commit v5 on v4

--- a/solution.py
+++ b/solution.py
@@ -539,9 +539,9 @@
         def start(self):
             block = self.buf.at[j]
             copies_out = [
+                send(block, block, dev(dc=1), self.near),
                 send(block, block, (s, zh * 4 + roles[1]), self.far + 1),
                 send(block, block, (s, zh * 4 + roles[2]), self.far + 2),
-                send(block, block, dev(dc=1), self.near),
             ]
             return copies_out
 
@@ -1127,6 +1127,8 @@
 
     scatter_n.reduce(0)
 
+    for ch in range(3):
+        total_q[ch].second()
     sums = [jnp.zeros((1, D), F32) for _ in range(2)]
     for m in range(4):
         lp = flip_l(m)
@@ -1162,8 +1164,6 @@
         GO[...] = GOF[...].astype(BF16)
         send(GO, XGO.at[1], dev(dzh=1), sem_go + 1)
 
-    for ch in range(3):
-        total_q[ch].second()
 
     bias_d = PV[7:8, :]
     sem_out, sem_in = slots(), slots()

time: 161 us -> 157 us (0.975)
  Pallas kernels: 160 us -> 156 us
    pallas_call x1, Pallas kernels: 157 us -> 153 us  [fused_shards(): pl.pallas_call(functools.partial(fused_kernel, COPIES), out_shape=(shape(...]
where the time goes in v5:
time: 157 us
  Pallas kernels  156 us (99%)
    pallas_call x1, Pallas kernels, fused_shards(): pl.pallas_call(functools.partial(fused_kernel, COPIES), out_shape=(shape(...  153 us

profile of v5, /device:TPU:1, one launch (start us, length us, event | category | flops | bytes accessed | tf_op | source)
XLA Modules:
  0.0 156.8 jit_solution(13860336946303050493)
XLA Ops:
  0.7 153.1 %shard_map.280 = (bf16[1,128,1024]{2,1,0:T(8,128)(2,1)}, bf16[1,128,1024]{2,1,0:T(8,128)(2,1)}, bf16[3,8,32,128]{3,2,1,0:T(8,128)(2,1)}, bf16[32,1024]{1,0:T(8,1...) custom-call(bf16[1,128,1024]{2,1,0:T(8,128)(2,1)} %refs_0_.1, ...), custom_call_target="tpu_custom_call" | custom-call | tf_op jit(solution)/shard_map/pallas_call | solution.py:1400
  153.8 2.9 %shard_map.281 = (bf16[1,128,1024]{2,1,0:T(8,128)(2,1)}, bf16[1,128,1024]{2,1,0:T(8,128)(2,1)}, f32[32]{0:T(128)}, f32[32]{0:T(128)}, f32[32,3072]{1,0:T(8,128)}...) custom-call(bf16[1,128,1024]{2,1,0:T(8,128)(2,1)} %get-tuple-element, ...), custom_call_target="tpu_custom_call" | custom-call | tf_op jit(solution)/shard_map/pallas_call | solution.py:1424

commit v6 on v5

--- a/solution.py
+++ b/solution.py
@@ -1217,22 +1217,6 @@
             def _():
                 send(TGO.at[slot], out_o, (x * 2 + y, zh * 4 + slot), sem_gs + slot)
 
-    scatter_n.finish()
-    for r in range(4):
-        rows = pl.ds(r * 32, 32)
-        grad = scatter_n.rows(rows)
-        normal, root, _ = norm_rows(X[j, rows].astype(F32), gain1, shift1)
-        BI[rows] = (N2F[rows] + norm_back(grad, normal, root, gain1)).astype(BF16)
-    put_input = move(BI, out_input.at[0], 9)
-
-    @pl.when(native)
-    def _():
-        put_input.start()
-
-    @pl.when(foreign)
-    def _():
-        send(BI, out_input.at[0], partner, sem_in)
-
     for ch in range(3):
         TQ[ch] = total_q[ch].result().astype(BF16)
         for dc, dl in group_masks:
@@ -1240,6 +1224,26 @@
     put_q = [move(TQ.at[ch, j], out_q.at[ch, j], 11 + ch) for ch in range(3)]
     for ch in range(3):
         put_q[ch].start()
+
+    for r in range(4):
+        rows = pl.ds(r * 32, 32)
+        normal, root, _ = norm_rows(X[j, rows].astype(F32), gain1, shift1)
+        XO[rows] = normal
+        RS_[rows] = jnp.broadcast_to(root, (32, LANES))
+    scatter_n.finish()
+    for r in range(4):
+        rows = pl.ds(r * 32, 32)
+        grad = scatter_n.rows(rows)
+        BI[rows] = (N2F[rows] + norm_back(grad, XO[rows], RS_[rows][:, 0:1], gain1)).astype(BF16)
+    put_input = move(BI, out_input.at[0], 9)
+
+    @pl.when(native)
+    def _():
+        put_input.start()
+
+    @pl.when(foreign)
+    def _():
+        send(BI, out_input.at[0], partner, sem_in)
 
     for dl in (1, 2, 3):
         arrive(SLR.at[dl], sem_v2 + dl)

time: 157 us -> 157 us (level)
  no operation moved by 1% of the time
where the time goes in v6:
time: 157 us
  Pallas kernels  156 us (99%)
    pallas_call x1, Pallas kernels, fused_shards(): pl.pallas_call(functools.partial(fused_kernel, COPIES), out_shape=(shape(...  153 us

profile of v6, /device:TPU:1, one launch (start us, length us, event | category | flops | bytes accessed | tf_op | source)
XLA Modules:
  0.0 156.9 jit_solution(16481642704944061391)
XLA Ops:
  0.7 153.2 %shard_map.280 = (bf16[1,128,1024]{2,1,0:T(8,128)(2,1)}, bf16[1,128,1024]{2,1,0:T(8,128)(2,1)}, bf16[3,8,32,128]{3,2,1,0:T(8,128)(2,1)}, bf16[32,1024]{1,0:T(8,1...) custom-call(bf16[1,128,1024]{2,1,0:T(8,128)(2,1)} %refs_0_.1, ...), custom_call_target="tpu_custom_call" | custom-call | tf_op jit(solution)/shard_map/pallas_call | solution.py:1404
  153.9 2.9 %shard_map.281 = (bf16[1,128,1024]{2,1,0:T(8,128)(2,1)}, bf16[1,128,1024]{2,1,0:T(8,128)(2,1)}, f32[32]{0:T(128)}, f32[32]{0:T(128)}, f32[32,3072]{1,0:T(8,128)}...) custom-call(bf16[1,128,1024]{2,1,0:T(8,128)(2,1)} %get-tuple-element, ...), custom_call_target="tpu_custom_call" | custom-call | tf_op jit(solution)/shard_map/pallas_call | solution.py:1428
